TPU v7x, 128 devices: a whole 4x4x4 slice. The times are simulated.
128 devices in a mesh: pulse: 8 (over z_hi, x), gate: 16 (over y, z_lo, core).
Axes of the slice: x: 4, y: 4, z: 4 (z_hi: 2, z_lo: 2; z = z_hi * 2 + z_lo), core: 2. Of those that a mesh axis runs over, the one named last changes fastest.
Arguments:
- echoes: bfloat16 [2, 8, 2048, 4096], P(None, None, 'pulse', 'gate'), may hold values from -6 to 6
- replica: bfloat16 [2, 256], replicated, may hold values from -4 to 4
- beam_weights: float32 [2, 2, 8, 2048], P(None, None, None, 'pulse'), may hold values from -1.5 to 1.5
- track_doppler: int32 [32768], P(('pulse', 'gate')), may hold values from 0 to 2047, as said below
- track_gate: int32 [32768], P(('pulse', 'gate')), may hold values from 0 to 4095, as said below
- track_owner: int32 [32768], P(('pulse', 'gate')), may hold values from 0 to 127, as said below
Outputs:
- track_tiles: float32 [81920, 1024], P(('pulse', 'gate'))
Inputs may be any that keep to these rules, and one draw needn't show every extreme that they name: `track_doppler`: row k lies in Doppler block (k // 256) // 16: its bin is in that block of 256 bins. `track_gate`: row k lies in range block (k // 256) % 16: its gate is in that block of 256 gates. `track_owner`: within each aligned block of 256 rows no owner appears more than 5 times, and in every draw some owner appears exactly 5 times in every block.
All inputs are finite; a program needn't handle non-finite values.
Results may differ from a plain program's by a relative error of at most 0.015.
Values may be sent and summed in bfloat16 or wider, within the bound.
A program may use at most 320 MiB of HBM per device.

v0:
```python
import math

import jax
import jax.numpy as jnp
from jax import lax
from jax.sharding import PartitionSpec as P

TILE = 16


def passed_along(value, axis, steps):
    count = lax.axis_size(axis)
    leading, last = (max(0, -steps), min(count, count - steps))
    return lax.ppermute(value, axis, [(source, source + steps) for source in range(leading, last)])


def extended_2(block, sides, width):
    for axis, dim in sides:
        count = lax.axis_size(axis)
        forward = [(i, i + 1) for i in range(count - 1)]
        backward = [(target, source) for source, target in forward]
        low = lax.ppermute(
            lax.slice_in_dim(block, block.shape[dim] - width, None, axis=dim), axis, forward
        )
        high = lax.ppermute(lax.slice_in_dim(block, 0, width, axis=dim), axis, backward)
        block = jnp.concatenate([low, block, high], axis=dim)
    return block


def compress_range(echoes, replica):
    chirp_len = replica.shape[1]
    gates = echoes.shape[3]
    echo_rim = passed_along(echoes, "gate", -1)
    extended = jnp.concatenate([echoes, echo_rim], axis=3)
    block_width = min(128, gates)
    window_span = block_width + chirp_len
    gate_lag = lax.broadcasted_iota(
        jnp.int32, (window_span, block_width), 0
    ) - lax.broadcasted_iota(jnp.int32, (window_span, block_width), 1)
    inside = (gate_lag >= 0) & (gate_lag < chirp_len)
    safe_lag = jnp.clip(gate_lag, 0, chirp_len - 1)
    nothing = jnp.zeros((), replica.dtype)
    real_tap = jnp.where(inside, jnp.take(replica[0], safe_lag), nothing)
    imag_tap = jnp.where(inside, jnp.take(replica[1], safe_lag), nothing)
    from_real = jnp.stack([real_tap, -imag_tap], axis=1)
    from_imag = jnp.stack([imag_tap, real_tap], axis=1)
    toeplitz = jnp.stack([from_real, from_imag], axis=0)
    range_scale = 1.0 / math.sqrt(2.0 * chirp_len)
    pieces = []
    for offset in range(0, gates, block_width):
        window = extended[:, :, :, offset : offset + window_span]
        products = jnp.einsum(
            "qcpw,qwso->scpo", window, toeplitz, preferred_element_type=jnp.float32
        )
        pieces.append((products * range_scale).astype(jnp.bfloat16))
    return jnp.concatenate(pieces, axis=3)


def phase_table(rows, cols, period):
    product = (
        lax.broadcasted_iota(jnp.int32, (rows, cols), 0)
        * lax.broadcasted_iota(jnp.int32, (rows, cols), 1)
        % period
    )
    angle = product.astype(jnp.float32) * (2.0 * math.pi / period)
    return (jnp.cos(angle), jnp.sin(angle))


def complex_table(size):
    cos_part, sin_part = phase_table(size, size, size)
    top_row = jnp.stack([cos_part, sin_part])
    low_row = jnp.stack([-sin_part, cos_part])
    return jnp.stack([top_row, low_row]).astype(jnp.bfloat16)


def doppler_transform(turned):
    channels, pulse_count, gates = (turned.shape[1], turned.shape[2], turned.shape[3])
    first = 1 << pulse_count.bit_length() // 2
    second = pulse_count // first
    parts = turned.reshape(2, channels, first, second, gates)
    f32 = jnp.float32
    section = jnp.einsum(
        "oiap,icpbg->ocabg", complex_table(first), parts, preferred_element_type=f32
    )
    section_real = section[0]
    section_imag = section[1]
    cos_twist, sin_twist = phase_table(first, second, pulse_count)
    cos_twist = cos_twist[None, :, :, None]
    sin_twist = sin_twist[None, :, :, None]
    twist_real = (section_real * cos_twist + section_imag * sin_twist).astype(jnp.bfloat16)
    twist_imag = (section_imag * cos_twist - section_real * sin_twist).astype(jnp.bfloat16)
    twisted = jnp.stack([twist_real, twist_imag])
    final = jnp.einsum(
        "oieb,icabg->oceag", complex_table(second), twisted, preferred_element_type=f32
    )
    norm_scale = 1.0 / math.sqrt(pulse_count)
    return (final * norm_scale).reshape(2, channels, pulse_count, gates).astype(jnp.bfloat16)


def local(echoes, replica, beam_weights, track_doppler, track_gate, track_owner):
    compressed = compress_range(echoes, replica)
    turned = lax.all_to_all(compressed, "pulse", split_axis=1, concat_axis=2, tiled=True)
    spectra = doppler_transform(turned)
    spectrum = lax.all_to_all(spectra, "pulse", split_axis=2, concat_axis=1, tiled=True)
    spec_real = spectrum[0].astype(jnp.float32)[None]
    spec_imag = spectrum[1].astype(jnp.float32)[None]
    weight_real = beam_weights[0][:, :, :, None]
    weight_imag = beam_weights[1][:, :, :, None]
    beam_real = jnp.sum(weight_real * spec_real - weight_imag * spec_imag, axis=1)
    beam_imag = jnp.sum(weight_real * spec_imag + weight_imag * spec_real, axis=1)
    beams = jnp.stack([beam_real, beam_imag])
    beam_count = beams.shape[1]
    framed = extended_2(beams.astype(jnp.bfloat16), (("pulse", 2), ("gate", 3)), TILE // 2).astype(
        beams.dtype
    )
    local_bin = track_doppler % beams.shape[2]
    local_gate = track_gate % beams.shape[3]
    zero_index = jnp.zeros((), jnp.int32)

    def cut_tile(doppler_bin, range_gate):
        starts = (zero_index, zero_index, doppler_bin, range_gate)
        return lax.dynamic_slice(framed, starts, (2, beam_count, TILE, TILE)).reshape(-1)

    tile_rows = jax.vmap(cut_tile)(local_bin, local_gate)
    pulse_devices = lax.axis_size("pulse")
    gate_devices = lax.axis_size("gate")
    owner_total = pulse_devices * gate_devices
    track_count = track_owner.shape[0]
    capacity = max(2, 5 * track_count // (2 * owner_total))
    owner_match = (
        track_owner[:, None] == jnp.arange(owner_total, dtype=jnp.int32)[None, :]
    ).astype(jnp.int32)
    running = jnp.cumsum(owner_match, axis=0, dtype=jnp.int32)
    slot_rank = jnp.sum(running * owner_match, axis=1, dtype=jnp.int32) - 1
    slot_index = track_owner * capacity + slot_rank
    features = tile_rows.shape[1]
    outgoing = (
        jnp.zeros((owner_total * capacity, features), jnp.float32).at[slot_index].set(tile_rows)
    )
    received = lax.all_to_all(
        outgoing.astype(jnp.bfloat16), ("pulse", "gate"), split_axis=0, concat_axis=0, tiled=True
    ).astype(outgoing.dtype)
    return received


def solution(mesh):
    return jax.shard_map(
        local,
        mesh=mesh,
        in_specs=(
            P(None, None, "pulse", "gate"),
            P(),
            P(None, None, None, "pulse"),
            P(("pulse", "gate")),
            P(("pulse", "gate")),
            P(("pulse", "gate")),
        ),
        out_specs=P(("pulse", "gate"), None),
        check_vma=False,
    )
```

profile of v0, /device:TPU:1, one launch (start us, length us, event | category | flops | bytes accessed | tf_op | source)
XLA Modules:
  0.0 960.4 jit_solution(13344692086269066765)
XLA Ops:
  0.0 3.5 fusion.62
  3.5 3.3 collective-permute-start
  7.1 287.1 %gather_fusion.1 = bf16[49152]{0:T(1024)(128)(2,1)S(1)} fusion(bf16[256]{0:T(256)(128)(2,1)S(1)} %get-tuple-element.9, s32[49152]{0:T(1024)S(1)} %bitcast_clamp_fusion), kind=kCustom, calls=%fused_computation.clone | custom fusion | bytes 393216 | tf_op jit(solution)/shard_map/jit(_take)/gather | solution.py:43
  294.3 287.1 %gather_fusion.2 = bf16[49152]{0:T(1024)(128)(2,1)S(1)} fusion(bf16[256]{0:T(256)(128)(2,1)S(1)} %get-tuple-element.8, s32[49152]{0:T(1024)S(1)} %bitcast_clamp_fusion), kind=kCustom, calls=%fused_computation.1.clone | custom fusion | bytes 393216 | tf_op jit(solution)/shard_map/jit(_take)/gather | solution.py:44
  581.7 3.2 constant_dynamic-update-slice_fusion
  584.9 3.1 fusion.10
  588.0 1.0 fusion.11
  589.1 0.1 pad_maximum_fusion
  589.2 1.5 copy.75
  590.7 7.4 all-to-all-start
  598.2 0.1 fusion.44
  598.4 0.2 negate_convert_fusion
  598.7 28.4 %all-to-all-done = bf16[2,8,256,256]{2,3,0,1:T(8,128)(2,1)} async-done(((bf16[2,8,256,256]{2,3,0,1:T(8,128)(2,1)}), bf16[2,8,256,256]{2,3,0,1:T(8,128)(2,1)}, u32[]{:S(2)}, u32[]{:S(2)}) %all-to-all-start) | async-done | bytes 2097184 | tf_op jit(solution)/shard_map/all_to_all | solution.py:102
  627.1 2.8 copy.76
  629.9 1.6 convolution_bitcast_fusion
  631.6 0.7 add_convert_fusion
  632.3 0.2 maximum_bitcast_fusion
  632.5 1.9 fusion.7
  634.5 1.2 copy.79
  635.7 14.0 %copy.80 = bf16[2,1,2048,256]{3,0,1,2:T(2,128)(2,1)} copy(bf16[2,1,2048,256]{3,2,0,1:T(8,128)(2,1)S(1)} %bitcast.122) | data formatting | bytes 4194304 | tf_op jit(solution)/shard_map/convert_element_type | solution.py:97
  649.7 9.2 all-to-all-start.1
  659.0 0.2 fusion.17
  659.3 0.2 fusion.18
  659.5 27.9 %all-to-all-done.1 = bf16[2,1,2048,256]{3,0,1,2:T(2,128)(2,1)S(1)} async-done(((bf16[2,1,2048,256]{3,0,1,2:T(2,128)(2,1)}), bf16[2,1,2048,256]{3,0,1,2:T(2,128)(2,1)S(1)}, u32[]{:S(2)}, u32[]{:S(2)}) %all-to-all-start.1) | async-done | bytes 2097184 | tf_op jit(solution)/shard_map/all_to_all | solution.py:104
  687.4 2.9 slice_convert_fusion.1
  690.3 0.1 copy.99
  690.6 1.6 subtract_reduce_fusion
  692.3 1.6 collective-permute-start.1
  693.9 1.3 collective-permute-start.2
  695.2 3.2 collective-permute-done.2
  698.4 0.1 fusion.63
  698.5 0.1 copy.101
  698.7 4.2 collective-permute-start.3
  702.9 0.1 copy.102
  703.1 2.4 collective-permute-start.4
  705.5 0.2 copy.83
  705.7 2.5 collective-permute-done.4
  708.2 0.2 copy.84
  708.4 0.5 maximum_convert_fusion
  708.9 64.3 %copy.85 = f32[2,2,272,272]{1,0,3,2:T(2,128)} copy(f32[2,2,272,272]{3,2,1,0:T(8,128)S(1)} %maximum_convert_fusion) | data formatting | bytes 2367488 | tf_op jit(solution)/shard_map/convert_element_type | solution.py:113
  773.1 77.3 %gather_fusion = f32[256,2,2,16,16]{2,1,4,3,0:T(2,128)} fusion(f32[2,2,272,272]{1,0,3,2:T(2,128)} %copy.85, s32[256]{0:T(256)S(1)} %fusion.55), kind=kCustom, calls=%fused_computation.2 | custom fusion | bytes 2101248 | tf_op jit(solution)/shard_map/vmap()/gather | solution.py:122
  850.4 55.3 %copy.86 = f32[256,2,2,16,16]{0,4,3,2,1:T(8,128)S(1)} copy(f32[256,2,2,16,16]{2,1,4,3,0:T(2,128)} %gather_fusion) | data formatting | bytes 2097152 | tf_op jit(solution)/shard_map/vmap()/gather | solution.py:122
  905.7 1.3 copy.87
  907.1 2.7 scatter_custom_fusion
  909.8 1.3 convert_element_type.167
  911.1 2.4 all_to_all.22
  913.5 43.0 %all_to_all.27 = bf16[128,5,1024]{2,1,0:T(8,128)(2,1)} all-to-all(bf16[128,5,1024]{2,1,0:T(8,128)(2,1)S(1)} %all_to_all.22), channel_id=1, replica_groups=mesh['pulse'=8,'gate'=16] {'pulse','gate'}, dimensions={0} | all-to-all | bytes 2621440 | tf_op jit(solution)/shard_map/all_to_all | solution.py:140
  956.5 3.9 reshape.262
  (41 shorter events, 1.4 us)
Async XLA Ops:
  0.0 7.0 copy-start.3
  3.5 578.3 %collective-permute-start = (bf16[2,8,256,256]{3,2,0,1:T(8,128)(2,1)S(1)}, bf16[2,8,256,256]{3,2,0,1:T(8,128)(2,1)}, u32[]{:S(2)}, u32[]{:S(2)}) collective-permute-start(bf16[2,8,256,256]{3,2,0,1:T(8,128)(2,1)S(1)} %get-tuple-element.14), channel_id=1, source_target_pairs={{1,0},{2,1},{3,2},{4,3},{5,4},{6,5},{7,6},{8,7},{9,8},{10,9},{11,1... | collective-permute-start | bytes 6291464 | tf_op jit(solution)/shard_map/ppermute | solution.py:14
  584.9 3.1 copy-start
  590.7 36.4 %all-to-all-start = ((bf16[2,8,256,256]{2,3,0,1:T(8,128)(2,1)}), bf16[2,8,256,256]{2,3,0,1:T(8,128)(2,1)}, u32[]{:S(2)}, u32[]{:S(2)}) async-start(bf16[2,8,256,256]{2,3,0,1:T(8,128)(2,1)} %copy.75), calls=%async_computation | async-start | bytes 4194304 | tf_op jit(solution)/shard_map/all_to_all | solution.py:102
  649.7 9.2 copy-start.2
  649.7 9.8 %copy-start.1 = (f32[2,2,8,256]{3,2,1,0:T(8,128)S(1)}, f32[2,2,8,256]{3,2,1,0:T(8,128)}, u32[]{:S(2)}) copy-start(f32[2,2,8,256]{3,2,1,0:T(8,128)} %param.10) | copy-start | bytes 98308
  649.7 37.7 %all-to-all-start.1 = ((bf16[2,1,2048,256]{3,0,1,2:T(2,128)(2,1)}), bf16[2,1,2048,256]{3,0,1,2:T(2,128)(2,1)S(1)}, u32[]{:S(2)}, u32[]{:S(2)}) async-start(bf16[2,1,2048,256]{3,0,1,2:T(2,128)(2,1)} %copy.80), calls=%async_computation.1 | async-start | bytes 4194304 | tf_op jit(solution)/shard_map/all_to_all | solution.py:104
  692.2 13.2 %copy-start.4 = (s32[256]{0:T(256)S(1)}, s32[256]{0:T(256)}, u32[]{:S(2)}) copy-start(s32[256]{0:T(256)} %param.11) | copy-start | bytes 3076
  692.3 13.2 %copy-start.5 = (s32[256]{0:T(256)S(1)}, s32[256]{0:T(256)}, u32[]{:S(2)}) copy-start(s32[256]{0:T(256)} %param.12) | copy-start | bytes 3076
  692.3 2.9 collective-permute-start.1
  693.9 4.5 collective-permute-start.2
  698.7 6.8 collective-permute-start.3
  703.1 5.1 collective-permute-start.4
where the time goes:
time: 962 us; the launch traced here: 960 us
  local copies, waits for them, and re-layouts  809 us (84%)
  waiting for transfers between devices  62 us (6%)
  blocking collectives  43 us (4%)
  starting transfers between devices  29.4 us (3%)
    gather x2, local copies, waits for them, and re-layouts, compress_range(): imag_tap = jnp.where(inside, jnp.take(replica[1], safe_lag), nothing)  287 us
    gather x2, local copies, waits for them, and re-layouts, compress_range(): real_tap = jnp.where(inside, jnp.take(replica[0], safe_lag), nothing)  287 us
    gather x2, local copies, waits for them, and re-layouts, cut_tile(): lax.dynamic_slice(framed, starts, (2, beam_count, TILE, TILE)).reshape(-1)  133 us
    convert_element_type x1, local copies, waits for them, and re-layouts, local(): extended_2(beams.astype(jnp.bfloat16), (('pulse', 2), ('gate', 3)), TILE...  64.3 us
    all_to_all x1, blocking collectives, local(): lax.all_to_all(outgoing.astype(jnp.bfloat16), ('pulse', 'gate'), split_ax...  43 us
    all_to_all x1, waiting for transfers between devices, local(): lax.all_to_all(compressed, 'pulse', split_axis=1, concat_axis=2, tiled=True)  28.4 us
    all_to_all x1, waiting for transfers between devices, local(): lax.all_to_all(spectra, 'pulse', split_axis=2, concat_axis=1, tiled=True)  27.9 us
  transfers between devices with their start and end apart: 7, of which 4 were waited for; matrix products, arithmetic and copies ran while one was open for 60% of the time, Pallas kernels for 0%

commit v1 on v0

v1 whole, which is shorter than its diff:
```python
import functools
import math

import jax
import jax.numpy as jnp
import numpy as np
from jax import lax
from jax.experimental import pallas as pl
from jax.experimental.pallas import tpu as pltpu
from jax.sharding import PartitionSpec as P

F32 = jnp.float32
BF16 = jnp.bfloat16
UNITS = 18
ROWS = 40
VMEM = pl.BlockSpec(memory_space=pltpu.VMEM)
SMEM = pl.BlockSpec(memory_space=pltpu.SMEM)


def tables():
    angle = 2.0 * np.pi * ((np.arange(256)[:, None] * np.arange(256)[None, :]) % 256) / 256.0
    cos, sin = np.cos(angle), np.sin(angle)
    dft = np.block([[cos, sin], [-sin, cos]]).astype(jnp.bfloat16)
    twist = 2.0 * np.pi * (np.arange(8)[:, None] * np.arange(256)[None, :]) / 2048.0
    scale = 1.0 / 1024.0
    return (
        dft,
        (np.cos(twist) * scale).astype(np.float32),
        (np.sin(twist) * scale).astype(np.float32),
    )


def cadd(a, b):
    return (a[0] + b[0], a[1] + b[1])


def csub(a, b):
    return (a[0] - b[0], a[1] - b[1])


def turn(a):
    return (a[1], -a[0])


def dft4(a):
    e0, e1 = cadd(a[0], a[2]), csub(a[0], a[2])
    f0, f1 = cadd(a[1], a[3]), turn(csub(a[1], a[3]))
    return [cadd(e0, f0), cadd(e1, f1), csub(e0, f0), csub(e1, f1)]


def dft8(x):
    root = math.sqrt(0.5)
    even = dft4([cadd(x[k], x[k + 4]) for k in range(4)])
    b = [csub(x[k], x[k + 4]) for k in range(4)]
    b1 = ((b[1][0] + b[1][1]) * root, (b[1][1] - b[1][0]) * root)
    b3 = ((b[3][1] - b[3][0]) * root, (b[3][0] + b[3][1]) * -root)
    odd = dft4([b[0], b1, turn(b[2]), b3])
    return [(even, odd)[d % 2][d // 2] for d in range(8)]


def doppler_channel(c, x_ref, w_ref, dft_ref, cos_ref, sin_ref, z_ref, acc_ref):
    for unit in range(2):
        for half in range(2):
            cols = slice(128 * half, 128 * half + 128)
            rows = slice(16 * unit, 16 * unit + 16)
            x = [
                tuple(x_ref[pb, q, c, rows, cols].astype(F32) for q in range(2)) for pb in range(8)
            ]
            for d, (re, im) in enumerate(dft8(x)):
                cos, sin = cos_ref[d : d + 1, cols], sin_ref[d : d + 1, cols]
                at = slice(128 * unit + 16 * d, 128 * unit + 16 * d + 16)
                z_ref[at, 128 * half : 128 * half + 128] = (re * cos + im * sin).astype(BF16)
                z_ref[at, 256 + 128 * half : 384 + 128 * half] = (im * cos - re * sin).astype(BF16)
    spec = lax.dot_general(
        dft_ref[...], z_ref[...], (((1,), (1,)), ((), ())), preferred_element_type=F32
    )
    lane = lax.broadcasted_iota(jnp.int32, (16, 16, 128), 2)
    keep = lane // 8 == lax.broadcasted_iota(jnp.int32, (16, 16, 128), 1)
    spread = (
        lax.broadcasted_iota(jnp.int32, (128, 128), 0) % 8
        == lax.broadcasted_iota(jnp.int32, (128, 128), 1) // 16
    )
    spread = jnp.where(spread, 1.0, 0.0).astype(BF16)
    for b in range(2):
        wide = []
        for q in range(2):
            w = jnp.where(keep, w_ref[(q * 2 + b) * 8 + c][:, None, :], 0.0).reshape(256, 128)
            high = w.astype(BF16)
            rest = w - high.astype(F32)
            mid = rest.astype(BF16)
            low = (rest - mid.astype(F32)).astype(BF16)
            wide.append(
                sum(jnp.dot(part, spread, preferred_element_type=F32) for part in (low, mid, high))
            )
        for unit in range(2):
            cols = slice(128 * unit, 128 * unit + 128)
            re, im = spec[:256, cols], spec[256:, cols]
            acc_ref[0, b, 8:264, cols] += wide[0] * re - wide[1] * im
            acc_ref[1, b, 8:264, cols] += wide[0] * im + wide[1] * re


def doppler_kernel(x_ref, w_ref, dft_ref, cos_ref, sin_ref, out_ref, z_ref, acc_ref):
    acc_ref[...] = jnp.zeros_like(acc_ref)

    def step(c, carry):
        doppler_channel(c, x_ref, w_ref, dft_ref, cos_ref, sin_ref, z_ref, acc_ref)
        return carry

    lax.fori_loop(0, 8, step, 0)
    for j in range(8):
        pack_block(j, acc_ref, out_ref)


def pack_block(j, acc_ref, out_ref):
    for unit in range(2):
        for q in range(2):
            both = jnp.concatenate(
                [
                    acc_ref[q, b, 32 * j + 7 : 32 * j + 7 + ROWS, 128 * unit : 128 * unit + 128]
                    for b in range(2)
                ],
                axis=0,
            )
            out_ref[j, unit, :, 128 * q : 128 * q + 128] = both.astype(BF16)


def taps_kernel(replica_ref, taps_ref):
    period = (
        lax.broadcasted_iota(jnp.int32, (16, 128), 0)
        == lax.broadcasted_iota(jnp.int32, (16, 128), 1) % 16
    )
    period = jnp.where(period, 1.0, 0.0).astype(F32)
    tables = []
    for q in range(2):
        row = jnp.concatenate(
            [replica_ref[q : q + 1, :].astype(F32), jnp.zeros((1, 128), F32)], axis=1
        )
        shifted = pltpu.roll(jnp.broadcast_to(row, (16, 384)), 0, 1, stride=1, stride_axis=0)
        tables.append(
            lax.dot_general(
                shifted.astype(BF16),
                period.astype(BF16),
                (((0,), (0,)), ((), ())),
                preferred_element_type=F32,
            )
        )
    lane = lax.broadcasted_iota(jnp.int32, (16, 128), 1) // 16
    for j in range(17):
        real, imag = (t[16 * j : 16 * j + 16] for t in tables)
        for d in range(8):
            keep = lane == d
            re, im = jnp.where(keep, real, 0.0), jnp.where(keep, imag, 0.0)
            from_real = jnp.concatenate([re, -im], axis=1).astype(BF16)
            from_imag = jnp.concatenate([im, re], axis=1).astype(BF16)
            taps_ref[j, 16 * d : 16 * d + 16, :] = from_real
            taps_ref[j, 128 + 16 * d : 144 + 16 * d, :] = from_imag


def compress(y_ref, taps_ref, sum_ref):
    depth = 2 * ROWS
    third = UNITS // 3

    def gates(block, first, count):
        x = jnp.concatenate(
            [
                y_ref[pl.ds(third * block + first + k, third)].reshape(third * depth, 256)
                for k in range(count)
            ],
            axis=1,
        )
        w = taps_ref[pl.ds(first, count)].reshape(256 * count, 256)
        return jnp.dot(x, w, preferred_element_type=F32)

    for block in range(3):
        rows = slice(block * third * depth, (block + 1) * third * depth)
        sum_ref[rows] = gates(block, 0, 5)
        for first in (5, 9, 13):
            sum_ref[rows] += gates(block, first, 4)


def frame(first_block, sum_ref, frame_ref):
    for unit in range(UNITS):
        for q in range(2):
            for b in range(2):
                for half in range(2):
                    start = (unit * 2 + b) * ROWS + half
                    value = sum_ref[start : start + 33, 128 * q : 128 * q + 128]
                    if unit == 0:
                        value = jnp.where(first_block, 0.0, value)
                    at = pl.ds(unit * 8 + q * 4 + b * 2 + half, 33, stride=8 * UNITS)
                    frame_ref[at, :] = value


def cut(base, shift, frame_ref):
    lane = lax.broadcasted_iota(jnp.int32, (8, 128), 1)
    gate = lane & 15
    gate_shift = shift & 15
    near_row, near_gate = lane >= shift - gate_shift, gate >= gate_shift
    f = [
        frame_ref[pl.ds(pl.multiple_of((base + step) * 8, 8), 8), :]
        for step in (0, 1, UNITS, UNITS + 1)
    ]
    z = jnp.where(
        near_row, jnp.where(near_gate, f[0], f[1]), jnp.where(near_gate, f[2], f[3])
    )
    return jnp.where(
        gate < 16 - gate_shift,
        pltpu.roll(z, (128 - shift) & 127, 1),
        pltpu.roll(z, (144 - shift) & 127, 1),
    )


def tiles_kernel(
    first_ref, base_ref, shift_ref, slot_ref, y_ref, taps_ref, out_ref, sum_ref, frame_ref, tile_ref
):
    compress(y_ref, taps_ref, sum_ref)
    frame(first_ref[0] > 0, sum_ref, frame_ref)
    tile_ref[...] = jnp.zeros_like(tile_ref)

    def step(k, carry):
        tile_ref[slot_ref[k]] = cut(base_ref[k], shift_ref[k], frame_ref)
        return carry

    lax.fori_loop(0, base_ref.shape[0], step, 0, unroll=8)
    out_ref[...] = tile_ref[...].reshape(out_ref.shape).astype(BF16)


def rows_kernel(in_ref, out_ref):
    slots = out_ref.shape[0]
    for k in range(8):
        out_ref[:, 128 * k : 128 * k + 128] = in_ref[pl.ds(k, slots, stride=8), :]


def shifted(value, steps):
    count = lax.axis_size("gate")
    pairs = [(i, i + steps) for i in range(count) if 0 <= i + steps < count]
    return lax.ppermute(value, "gate", pairs)


def params(mib, **more):
    return pltpu.CompilerParams(vmem_limit_bytes=mib << 20, **more)


def local(echoes, replica, beam_weights, track_doppler, track_gate, track_owner):
    pulse_devices, gate_devices = lax.axis_size("pulse"), lax.axis_size("gate")
    owners = pulse_devices * gate_devices
    tracks = track_owner.shape[0]
    capacity = 5
    dft, cos, sin = tables()

    strips = jnp.transpose(echoes, (3, 0, 1, 2)).reshape(8, 32, 2, 8, 256).transpose(0, 2, 3, 1, 4)
    gathered = lax.all_to_all(strips, "pulse", split_axis=0, concat_axis=0, tiled=True)
    weights = lax.all_gather(beam_weights, "pulse", axis=3, tiled=True).reshape(32, 16, 128)
    taps = pl.pallas_call(
        taps_kernel,
        out_shape=jax.ShapeDtypeStruct((17, 256, 256), BF16),
        in_specs=[VMEM],
        out_specs=VMEM,
        compiler_params=params(24),
        cost_estimate=pl.CostEstimate(flops=10**7, bytes_accessed=2**22, transcendentals=0),
    )(replica)

    blocks = pl.pallas_call(
        doppler_kernel,
        out_shape=jax.ShapeDtypeStruct((8, 2, 2 * ROWS, 256), BF16),
        in_specs=[VMEM] * 5,
        out_specs=VMEM,
        scratch_shapes=[pltpu.VMEM((256, 512), BF16), pltpu.VMEM((2, 2, 272, 256), F32)],
        compiler_params=params(24),
    )(gathered, weights, jnp.asarray(dft), jnp.asarray(cos), jnp.asarray(sin))
    own = lax.all_to_all(blocks, "pulse", split_axis=0, concat_axis=0, tiled=True).reshape(
        16, 2 * ROWS, 256
    )
    y = jnp.concatenate(
        [shifted(own[15:], 1), own, shifted(own, -1), shifted(own[:1], -2)], axis=0
    )

    row_in, gate_in = track_doppler % 256, track_gate % 256 + 8
    base = row_in // 8 * UNITS + gate_in // 16
    shift = row_in % 8 * 16 + gate_in % 16
    order = jnp.arange(tracks, dtype=jnp.int32)
    earlier = (track_owner[:, None] == track_owner[None, :]) & (order[None, :] < order[:, None])
    rank = jnp.sum(earlier.astype(jnp.int32), axis=1, dtype=jnp.int32)
    slot = track_owner * capacity + rank
    first = (lax.axis_index("gate") == 0).astype(jnp.int32).reshape(1)

    outgoing = pl.pallas_call(
        tiles_kernel,
        out_shape=jax.ShapeDtypeStruct((owners, capacity * 8, 128), BF16),
        in_specs=[SMEM] * 4 + [VMEM] * 2,
        out_specs=VMEM,
        scratch_shapes=[
            pltpu.VMEM((UNITS * 2 * ROWS, 256), F32),
            pltpu.VMEM((33 * UNITS * 8, 128), F32),
            pltpu.VMEM((owners * capacity, 8, 128), F32),
        ],
        compiler_params=params(32),
    )(first, base, shift, slot, y, taps)
    received = lax.all_to_all(
        outgoing, ("pulse", "gate"), split_axis=0, concat_axis=0, tiled=True
    )
    wide = received.reshape(owners * capacity * 8, 128).astype(F32)
    return pl.pallas_call(
        rows_kernel,
        out_shape=jax.ShapeDtypeStruct((owners * capacity, 1024), F32),
        in_specs=[VMEM],
        out_specs=VMEM,
        compiler_params=params(16),
    )(wide)


def solution(mesh):
    return jax.shard_map(
        local,
        mesh=mesh,
        in_specs=(
            P(None, None, "pulse", "gate"),
            P(),
            P(None, None, None, "pulse"),
            P(("pulse", "gate")),
            P(("pulse", "gate")),
            P(("pulse", "gate")),
        ),
        out_specs=P(("pulse", "gate"), None),
        check_vma=False,
    )
```

time: 962 us -> 142 us (0.15)
  local copies, waits for them, and re-layouts: 809 us -> 5.53 us
  waiting for transfers between devices: 62 us -> 5.46 us
  blocking collectives: 43 us -> 90.5 us
  Pallas kernels: 0 us -> 16.9 us
    gather x6 -> x0, local copies, waits for them, and re-layouts: 707 us -> none  [the longest x2 287 us: compress_range(): imag_tap = jnp.where(inside, jnp.take(replica[1], safe_lag), nothing)]
    convert_element_type x4 -> x0, local copies, waits for them, and re-layouts: 83.4 us -> none  [the longest x1 64.3 us: local(): extended_2(beams.astype(jnp.bfloat16), (('pulse', 2), ('gate', 3)), TILE...]
    all_to_all x2 -> x1, waiting for transfers between devices: 56.3 us -> 0.01 us  [local(): lax.all_to_all(strips, 'pulse', split_axis=0, concat_axis=0, tiled=True)]
    all_gather x0 -> x1, blocking collectives: none -> 50.1 us  [local(): lax.all_gather(beam_weights, 'pulse', axis=3, tiled=True)]
    pallas_call x0 -> x4, Pallas kernels: none -> 16.9 us  [the longest x1 7.94 us: local(): pl.pallas_call(tiles_kernel, out_shape=jax.ShapeDtypeStruct((owners, capa...]
    all_to_all x1 -> x2, blocking collectives: 43 us -> 40.4 us  [the longest x1 28.1 us: local(): lax.all_to_all(outgoing, ('pulse', 'gate'), split_axis=0, concat_axis=0,...]
  transfers between devices with their start and end apart: 7 -> 4, of which waited for: 4 -> 1; matrix products, arithmetic and copies ran while one was open for 60% -> 0% of each run, Pallas kernels for 0% -> 0%
where the time goes in v1:
time: 142 us
  blocking collectives  90.5 us (64%)
  starting transfers between devices  22.5 us (16%)
  Pallas kernels  16.9 us (12%)
  local copies, waits for them, and re-layouts  5.53 us (4%)
  waiting for transfers between devices  5.46 us (4%)
    all_gather x1, blocking collectives, local(): lax.all_gather(beam_weights, 'pulse', axis=3, tiled=True)  50.1 us
    all_to_all x1, blocking collectives, local(): lax.all_to_all(outgoing, ('pulse', 'gate'), split_axis=0, concat_axis=0,...  28.1 us
    ppermute x3, starting transfers between devices, shifted(): return lax.ppermute(value, 'gate', pairs)  14.2 us
    all_to_all x1, blocking collectives, local(): lax.all_to_all(blocks, 'pulse', split_axis=0, concat_axis=0, tiled=True)  12.3 us
    all_to_all x1, starting transfers between devices, local(): lax.all_to_all(strips, 'pulse', split_axis=0, concat_axis=0, tiled=True)  8.31 us
    pallas_call x1, Pallas kernels, local(): pl.pallas_call(tiles_kernel, out_shape=jax.ShapeDtypeStruct((owners, capa...  7.94 us
    pallas_call x1, Pallas kernels, local(): pl.pallas_call(doppler_kernel, out_shape=jax.ShapeDtypeStruct((8, 2, 2 *...  6.38 us
    ppermute x3, waiting for transfers between devices, shifted(): return lax.ppermute(value, 'gate', pairs)  5.46 us
  transfers between devices with their start and end apart: 4, of which 1 were waited for; matrix products, arithmetic and copies ran while one was open for 0% of the time, Pallas kernels for 0%

profile of v1, /device:TPU:1, one launch (start us, length us, event | category | flops | bytes accessed | tf_op | source)
XLA Modules:
  0.0 141.6 jit_solution(11832110986015490160)
XLA Ops:
  0.0 3.3 %copy.12 = bf16[2,8,256,256]{2,1,0,3:T(8,128)(2,1)S(1)} copy(bf16[2,8,256,256]{3,2,1,0:T(8,128)(2,1)} %param.9) | data formatting | bytes 4194304 | tf_op args[0]
  3.3 2.1 %copy.16 = bf16[8,32,2,8,256]{4,1,3,2,0:T(8,128)(2,1)} copy(bf16[8,32,2,8,256]{4,3,2,1,0:T(8,128)(2,1)S(1)} %bitcast.17) | data formatting | bytes 4194304 | tf_op jit(solution)/shard_map/reshape | solution.py:251
  5.4 0.0 copy-start.4
  5.5 0.0 copy-start
  5.5 0.0 copy-start.1
  5.5 0.0 copy-start.2
  5.5 8.3 %all-to-all-start = ((bf16[8,2,8,32,256]{4,3,2,1,0:T(8,128)(2,1)}), bf16[8,2,8,32,256]{4,3,2,1,0:T(8,128)(2,1)S(1)}, u32[]{:S(2)}, u32[]{:S(2)}) async-start(bf16[8,2,8,32,256]{4,3,2,1,0:T(8,128)(2,1)} %bitcast.16), calls=%async_computation | async-start | bytes 4194304 | tf_op jit(solution)/shard_map/all_to_all | solution.py:252
  13.8 0.0 copy-done.4
  13.8 50.1 %all_gather.3 = f32[2,2,8,2048]{3,2,1,0:T(8,128)S(1)} all-gather(f32[2,2,8,256]{3,2,1,0:T(8,128)S(1)} %copy-done.4), channel_id=1, replica_groups=mesh['pulse'=8,'gate'=16] {'pulse'}, dimensions={3}, use_global_device_ids=true | all-gather | bytes 294912 | tf_op jit(solution)/shard_map/all_gather | solution.py:253
  63.9 0.0 all-to-all-done.x_ref
  63.9 0.0 copy-done
  63.9 0.0 copy-done.1
  64.0 0.0 copy-done.2
  64.0 0.0 copy-start.5
  64.0 6.4 %shard_map.91 = bf16[8,2,80,256]{3,2,1,0:T(8,128)(2,1)S(1)} custom-call(bf16[8,2,8,32,256]{4,3,2,1,0:T(8,128)(2,1)S(1)} %all-to-all-done.x_ref, f32[32,16,128]{2,1,0:T(8,128)S(1)} %bitcast.15, bf16[512,512]{1,0:T(8,128)(2,1)S(1)} %copy-done, f32[8,256]{1,0:T(8,128)S(1)} %copy-done.2, f32[8,256]{1,0:T(8,128)S(1)} %copy-done.1), custom_call_target="tpu_custom_call" | custom-call | tf_op jit(solution)/shard_map/pallas_call | solution.py:263
  70.4 0.0 copy-start.6
  70.4 0.0 copy-start.7
  70.4 0.0 copy-start.3
  70.4 12.3 %all_to_all.15 = bf16[8,2,80,256]{3,2,1,0:T(8,128)(2,1)S(1)} all-to-all(bf16[8,2,80,256]{3,2,1,0:T(8,128)(2,1)S(1)} %shard_map.91), channel_id=1, replica_groups=mesh['pulse'=8,'gate'=16] {'pulse'}, dimensions={0} | all-to-all | bytes 1310720 | tf_op jit(solution)/shard_map/all_to_all | solution.py:271
  82.7 10.3 %collective-permute-start.1 = (bf16[16,80,256]{2,1,0:T(8,128)(2,1)S(1)}, bf16[16,80,256]{2,1,0:T(8,128)(2,1)S(1)}, u32[]{:S(2)}, u32[]{:S(2)}) collective-permute-start(bf16[16,80,256]{2,1,0:T(8,128)(2,1)S(1)} %bitcast.18), channel_id=1, source_target_pairs={{1,0},{2,1},{3,2},{4,3},{5,4},{6,5},{7,6},{8,7},{9,8},{10,9},{11,1... | collective-permute-start | bytes 1966088 | tf_op jit(solution)/shard_map/ppermute | solution.py:237
  93.0 0.0 copy-done.5
  93.1 0.2 convert_reduce_fusion
  93.2 2.5 %collective-permute-start = (bf16[1,80,256]{2,1,0:T(8,128)(2,1)S(1)}, bf16[1,80,256]{2,1,0:T(8,128)(2,1)S(1)}, u32[]{:S(2)}, u32[]{:S(2)}) collective-permute-start(bf16[1,80,256]{2,1,0:T(8,128)(2,1)S(1)} %get-tuple-element.5), channel_id=1, source_target_pairs={{0,1},{1,2},{2,3},{3,4},{4,5},{5,6},{6,7},{7,8},{8,9},{9,10},{10,1... | collective-permute-start | bytes 122888 | tf_op jit(solution)/shard_map/ppermute | solution.py:237
  95.8 1.3 collective-permute-start.2
  97.1 0.0 copy-done.6
  97.1 0.0 copy-done.7
  97.2 0.0 copy-done.3
  97.2 0.5 shard_map.92.taps_ref
  97.6 5.5 %collective-permute-done = bf16[1,80,256]{2,1,0:T(8,128)(2,1)S(1)} collective-permute-done((bf16[1,80,256]{2,1,0:T(8,128)(2,1)S(1)}, bf16[1,80,256]{2,1,0:T(8,128)(2,1)S(1)}, u32[]{:S(2)}, u32[]{:S(2)}) %collective-permute-start) | collective-permute-done | bytes 40992 | tf_op jit(solution)/shard_map/ppermute | solution.py:237
  103.1 0.0 collective-permute-done.2
  103.1 0.0 collective-permute-done.1
  103.1 0.2 pad_maximum_fusion.y_ref
  103.3 7.9 %shard_map.93 = bf16[128,40,128]{2,1,0:T(8,128)(2,1)S(1)} custom-call(s32[1]{0:T(128)} %bitcast.first_ref, s32[256]{0:T(256)S(1)} %get-tuple-element.8.base_ref, s32[256]{0:T(256)S(1)} %get-tuple-element.7.shift_ref, s32[256]{0:T(256)S(1)} %get-tuple-element.9.slot_ref, bf16[34,80,256]{2,1,0:T(8,128)(2,1)S(1)} %pad_maximum_fusion.y_ref, ...), custom_call_target="tpu_custom_call" | custom-call | tf_op jit(solution)/shard_map/pallas_call | solution.py:287
  111.2 28.1 %all_to_all.16 = bf16[128,40,128]{2,1,0:T(8,128)(2,1)S(1)} all-to-all(bf16[128,40,128]{2,1,0:T(8,128)(2,1)S(1)} %shard_map.93), channel_id=1, replica_groups=mesh['pulse'=8,'gate'=16] {'pulse','gate'}, dimensions={0} | all-to-all | bytes 2621440 | tf_op jit(solution)/shard_map/all_to_all | solution.py:299
  139.3 0.3 bitcast_convert_fusion.in_ref
  139.5 2.1 %shard_map.94 = f32[640,1024]{1,0:T(8,128)} custom-call(f32[5120,128]{1,0:T(8,128)S(1)} %bitcast_convert_fusion.in_ref), custom_call_target="tpu_custom_call" | custom-call | tf_op jit(solution)/shard_map/pallas_call | solution.py:303
  (3 shorter events, 0.1 us)
Async XLA Ops:
  5.4 8.3 %copy-start.4 = (f32[2,2,8,256]{3,2,1,0:T(8,128)S(1)}, f32[2,2,8,256]{3,2,1,0:T(8,128)}, u32[]{:S(2)}) copy-start(f32[2,2,8,256]{3,2,1,0:T(8,128)} %param.11) | copy-start | bytes 98308
  5.5 58.5 %copy-start = (bf16[512,512]{1,0:T(8,128)(2,1)S(1)}, bf16[512,512]{1,0:T(8,128)(2,1)}, u32[]{:S(2)}) copy-start(bf16[512,512]{1,0:T(8,128)(2,1)} %constant.81.clone.dft_ref) | copy-start | bytes 1572868
  5.5 58.5 %copy-start.1 = (f32[8,256]{1,0:T(8,128)S(1)}, f32[8,256]{1,0:T(8,128)}, u32[]{:S(2)}) copy-start(f32[8,256]{1,0:T(8,128)} %constant.83.clone.sin_ref) | copy-start | bytes 24580
  5.5 58.5 %copy-start.2 = (f32[8,256]{1,0:T(8,128)S(1)}, f32[8,256]{1,0:T(8,128)}, u32[]{:S(2)}) copy-start(f32[8,256]{1,0:T(8,128)} %constant.82.clone.cos_ref) | copy-start | bytes 24580
  5.5 58.5 %all-to-all-start = ((bf16[8,2,8,32,256]{4,3,2,1,0:T(8,128)(2,1)}), bf16[8,2,8,32,256]{4,3,2,1,0:T(8,128)(2,1)S(1)}, u32[]{:S(2)}, u32[]{:S(2)}) async-start(bf16[8,2,8,32,256]{4,3,2,1,0:T(8,128)(2,1)} %bitcast.16), calls=%async_computation | async-start | bytes 4194304 | tf_op jit(solution)/shard_map/all_to_all | solution.py:252
  64.0 29.1 %copy-start.5 = (s32[256]{0:T(256)S(1)}, s32[256]{0:T(256)}, u32[]{:S(2)}) copy-start(s32[256]{0:T(256)} %param.14) | copy-start | bytes 3076
  70.4 26.7 %copy-start.6 = (s32[256]{0:T(256)S(1)}, s32[256]{0:T(256)}, u32[]{:S(2)}) copy-start(s32[256]{0:T(256)} %param.12) | copy-start | bytes 3076
  70.4 26.7 %copy-start.7 = (s32[256]{0:T(256)S(1)}, s32[256]{0:T(256)}, u32[]{:S(2)}) copy-start(s32[256]{0:T(256)} %param.13) | copy-start | bytes 3076
  70.4 26.8 %copy-start.3 = (bf16[2,256]{1,0:T(2,128)(2,1)S(1)}, bf16[2,256]{1,0:T(2,128)(2,1)}, u32[]{:S(2)}) copy-start(bf16[2,256]{1,0:T(2,128)(2,1)} %replica_ref.1) | copy-start | bytes 3076
  82.7 20.4 %collective-permute-start.1 = (bf16[16,80,256]{2,1,0:T(8,128)(2,1)S(1)}, bf16[16,80,256]{2,1,0:T(8,128)(2,1)S(1)}, u32[]{:S(2)}, u32[]{:S(2)}) collective-permute-start(bf16[16,80,256]{2,1,0:T(8,128)(2,1)S(1)} %bitcast.18), channel_id=1, source_target_pairs={{1,0},{2,1},{3,2},{4,3},{5,4},{6,5},{7,6},{8,7},{9,8},{10,9},{11,1... | collective-permute-start | bytes 1966088 | tf_op jit(solution)/shard_map/ppermute | solution.py:237
  93.2 9.8 %collective-permute-start = (bf16[1,80,256]{2,1,0:T(8,128)(2,1)S(1)}, bf16[1,80,256]{2,1,0:T(8,128)(2,1)S(1)}, u32[]{:S(2)}, u32[]{:S(2)}) collective-permute-start(bf16[1,80,256]{2,1,0:T(8,128)(2,1)S(1)} %get-tuple-element.5), channel_id=1, source_target_pairs={{0,1},{1,2},{2,3},{3,4},{4,5},{5,6},{6,7},{7,8},{8,9},{9,10},{10,1... | collective-permute-start | bytes 122888 | tf_op jit(solution)/shard_map/ppermute | solution.py:237
  95.8 7.3 %collective-permute-start.2 = (bf16[1,80,256]{2,1,0:T(8,128)(2,1)S(1)}, bf16[1,80,256]{2,1,0:T(8,128)(2,1)S(1)}, u32[]{:S(2)}, u32[]{:S(2)}) collective-permute-start(bf16[1,80,256]{2,1,0:T(8,128)(2,1)S(1)} %get-tuple-element.6), channel_id=1, source_target_pairs={{2,0},{3,1},{4,2},{5,3},{6,4},{7,5},{8,6},{9,7},{10,8},{11,9},{12,... | collective-permute-start | bytes 122888 | tf_op jit(solution)/shard_map/ppermute | solution.py:237

commit v2 on v1

--- a/solution.py
+++ b/solution.py
@@ -58,14 +58,12 @@
     return [(even, odd)[d % 2][d // 2] for d in range(8)]
 
 
-def doppler_channel(c, x_ref, w_ref, dft_ref, cos_ref, sin_ref, z_ref, acc_ref):
+def doppler_channel(c, x_ref, wide_ref, dft_ref, cos_ref, sin_ref, z_ref, acc_ref):
     for unit in range(2):
         for half in range(2):
             cols = slice(128 * half, 128 * half + 128)
             rows = slice(16 * unit, 16 * unit + 16)
-            x = [
-                tuple(x_ref[pb, q, c, rows, cols].astype(F32) for q in range(2)) for pb in range(8)
-            ]
+            x = [tuple(x_ref(pb, q)[rows, cols].astype(F32) for q in range(2)) for pb in range(8)]
             for d, (re, im) in enumerate(dft8(x)):
                 cos, sin = cos_ref[d : d + 1, cols], sin_ref[d : d + 1, cols]
                 at = slice(128 * unit + 16 * d, 128 * unit + 16 * d + 16)
@@ -74,41 +72,36 @@
     spec = lax.dot_general(
         dft_ref[...], z_ref[...], (((1,), (1,)), ((), ())), preferred_element_type=F32
     )
-    lane = lax.broadcasted_iota(jnp.int32, (16, 16, 128), 2)
-    keep = lane // 8 == lax.broadcasted_iota(jnp.int32, (16, 16, 128), 1)
+    for b in range(2):
+        real, imag = (wide_ref[(q * 2 + b) * 8 + c] for q in range(2))
+        for unit in range(2):
+            cols = slice(128 * unit, 128 * unit + 128)
+            re, im = spec[:256, cols], spec[256:, cols]
+            acc_ref[0, b, 8:264, cols] += real * re - imag * im
+            acc_ref[1, b, 8:264, cols] += real * im + imag * re
+
+
+def widen(i, weight_ref, wide_ref):
+    lane = lax.broadcasted_iota(jnp.int32, (16, 128), 1)
+    keep = lane // 8 == lax.broadcasted_iota(jnp.int32, (16, 128), 0)
     spread = (
         lax.broadcasted_iota(jnp.int32, (128, 128), 0) % 8
         == lax.broadcasted_iota(jnp.int32, (128, 128), 1) // 16
     )
     spread = jnp.where(spread, 1.0, 0.0).astype(BF16)
-    for b in range(2):
-        wide = []
-        for q in range(2):
-            w = jnp.where(keep, w_ref[(q * 2 + b) * 8 + c][:, None, :], 0.0).reshape(256, 128)
-            high = w.astype(BF16)
-            rest = w - high.astype(F32)
-            mid = rest.astype(BF16)
-            low = (rest - mid.astype(F32)).astype(BF16)
-            wide.append(
-                sum(jnp.dot(part, spread, preferred_element_type=F32) for part in (low, mid, high))
-            )
-        for unit in range(2):
-            cols = slice(128 * unit, 128 * unit + 128)
-            re, im = spec[:256, cols], spec[256:, cols]
-            acc_ref[0, b, 8:264, cols] += wide[0] * re - wide[1] * im
-            acc_ref[1, b, 8:264, cols] += wide[0] * im + wide[1] * re
-
-
-def doppler_kernel(x_ref, w_ref, dft_ref, cos_ref, sin_ref, out_ref, z_ref, acc_ref):
-    acc_ref[...] = jnp.zeros_like(acc_ref)
-
-    def step(c, carry):
-        doppler_channel(c, x_ref, w_ref, dft_ref, cos_ref, sin_ref, z_ref, acc_ref)
-        return carry
-
-    lax.fori_loop(0, 8, step, 0)
-    for j in range(8):
-        pack_block(j, acc_ref, out_ref)
+    w = jnp.concatenate(
+        [
+            jnp.where(keep, weight_ref[source, half, pl.ds(i, 1), :], 0.0)
+            for source in range(8)
+            for half in range(2)
+        ],
+        axis=0,
+    )
+    high = w.astype(BF16)
+    rest = w - high.astype(F32)
+    mid = rest.astype(BF16)
+    low = (rest - mid.astype(F32)).astype(BF16)
+    wide_ref[i] = sum(jnp.dot(part, spread, preferred_element_type=F32) for part in (low, mid, high))
 
 
 def pack_block(j, acc_ref, out_ref):
@@ -121,10 +114,10 @@
                 ],
                 axis=0,
             )
-            out_ref[j, unit, :, 128 * q : 128 * q + 128] = both.astype(BF16)
-
-
-def taps_kernel(replica_ref, taps_ref):
+            out_ref[unit, :, 128 * q : 128 * q + 128] = both.astype(BF16)
+
+
+def make_taps(replica_ref, taps_ref):
     period = (
         lax.broadcasted_iota(jnp.int32, (16, 128), 0)
         == lax.broadcasted_iota(jnp.int32, (16, 128), 1) % 16
@@ -210,11 +203,296 @@
     )
 
 
-def tiles_kernel(
-    first_ref, base_ref, shift_ref, slot_ref, y_ref, taps_ref, out_ref, sum_ref, frame_ref, tile_ref
+CHUNKS = 4
+PER = 8 // CHUNKS
+
+
+def beams_kernel(
+    echo_ref,
+    weight_ref,
+    replica_ref,
+    dft_ref,
+    cos_ref,
+    sin_ref,
+    frame_ref,
+    out_strip,
+    in_strip,
+    all_weights,
+    wide_ref,
+    z_ref,
+    acc_ref,
+    out_block,
+    y_ref,
+    taps_ref,
+    sum_ref,
+    strip_sent,
+    strip_here,
+    strip_own,
+    weight_sent,
+    weight_here,
+    block_sent,
+    block_here,
+    halo_sent,
+    halo_here,
+    edge_sent,
+    edge_here,
 ):
+    me, g = lax.axis_index("pulse"), lax.axis_index("gate")
+    gates = lax.axis_size("gate")
+    barrier = pltpu.get_barrier_semaphore()
+
+    def at(pulse, gate):
+        return dict(device_id=(pulse, gate), device_id_type=pl.DeviceIdType.MESH)
+
+    def peer(k):
+        return lax.rem(me + k, 8)
+
+    for k in range(1, 8):
+        pl.semaphore_signal(barrier, inc=1, **at(peer(k), g))
+    near = jnp.int32(7)
+    for step in (-2, -1, 1, 2):
+        there = (g + step >= 0) & (g + step < gates)
+        near += there.astype(jnp.int32)
+
+        @pl.when(there)
+        def _():
+            pl.semaphore_signal(barrier, inc=1, **at(me, g + step))
+
+    def strip(chunk, target, source):
+        return pltpu.make_async_remote_copy(
+            src_ref=out_strip.at[chunk, target],
+            dst_ref=in_strip.at[chunk, source],
+            send_sem=strip_sent.at[chunk, target],
+            recv_sem=strip_here.at[chunk, source],
+            **at(target, g),
+        )
+
+    def own_strip(chunk):
+        return pltpu.make_async_copy(
+            out_strip.at[chunk, me], in_strip.at[chunk, me], strip_own.at[chunk]
+        )
+
+    def weight(target, source):
+        return pltpu.make_async_remote_copy(
+            src_ref=weight_ref,
+            dst_ref=all_weights.at[source],
+            send_sem=weight_sent.at[target],
+            recv_sem=weight_here.at[source],
+            **at(target, g),
+        )
+
+    def block(target, source):
+        return pltpu.make_async_remote_copy(
+            src_ref=out_block.at[target],
+            dst_ref=y_ref.at[pl.ds(1 + 2 * source, 2)],
+            send_sem=block_sent.at[target],
+            recv_sem=block_here.at[source],
+            **at(target, g),
+        )
+
+    def halo(source):
+        return pltpu.make_async_remote_copy(
+            src_ref=y_ref.at[pl.ds(1 + 2 * source, 2)],
+            dst_ref=y_ref.at[pl.ds(17 + 2 * source, 2)],
+            send_sem=halo_sent.at[source],
+            recv_sem=halo_here.at[source],
+            **at(me, g - 1),
+        )
+
+    def edge(which):
+        return pltpu.make_async_remote_copy(
+            src_ref=y_ref.at[(1, 16)[which]],
+            dst_ref=y_ref.at[(33, 0)[which]],
+            send_sem=edge_sent.at[which],
+            recv_sem=edge_here.at[which],
+            **at(me, (g - 2, g + 1)[which]),
+        )
+
+    def turn_chunk(chunk):
+        for c in range(PER):
+            for q in range(2):
+                turned = echo_ref[q, chunk * PER + c].T
+                out_strip[chunk, :, q, c] = turned.reshape(8, 32, 256)
+
+    def send_chunk(chunk):
+        for k in range(1, 8):
+            strip(chunk, peer(k), me).start()
+        own_strip(chunk).start()
+
+    turn_chunk(0)
+    pl.semaphore_wait(barrier, near)
+    send_chunk(0)
+    for k in range(1, 8):
+        weight(peer(k), me).start()
+
+    def turn_and_send(chunk, carry):
+        turn_chunk(chunk)
+        send_chunk(chunk)
+        return carry
+
+    lax.fori_loop(1, CHUNKS, turn_and_send, 0)
+
+    all_weights[me] = weight_ref[...]
+    acc_ref[...] = jnp.zeros_like(acc_ref)
+    nothing = jnp.zeros((2 * ROWS, 256), BF16)
+
+    @pl.when(g == 0)
+    def _():
+        y_ref[0] = nothing
+
+    @pl.when(g == gates - 1)
+    def _():
+        for unit in range(17, 33):
+            y_ref[unit] = nothing
+
+    @pl.when(g >= gates - 2)
+    def _():
+        y_ref[33] = nothing
+
+    make_taps(replica_ref, taps_ref)
+    for k in range(1, 8):
+        weight(me, peer(k)).wait_recv()
+
+    def widen_step(i, carry):
+        widen(i, all_weights, wide_ref)
+        return carry
+
+    lax.fori_loop(0, 32, widen_step, 0)
+
+    def doppler_chunk(chunk, carry):
+        own_strip(chunk).wait()
+        for k in range(1, 8):
+            strip(chunk, me, peer(k)).wait_recv()
+
+        def one(c, inner):
+            doppler_channel(
+                chunk * PER + c,
+                lambda pb, q: in_strip.at[chunk, pb, q, c],
+                wide_ref,
+                dft_ref,
+                cos_ref,
+                sin_ref,
+                z_ref,
+                acc_ref,
+            )
+            return inner
+
+        return lax.fori_loop(0, PER, one, carry)
+
+    lax.fori_loop(0, CHUNKS, doppler_chunk, 0)
+
+    for j in range(8):
+
+        @pl.when(me == j)
+        def _():
+            pack_block(j, acc_ref, y_ref.at[pl.ds(1 + 2 * j, 2)])
+
+        @pl.when(me != j)
+        def _():
+            pack_block(j, acc_ref, out_block.at[j])
+            block(j, me).start()
+
+    def pass_on(source):
+        @pl.when(g > 0)
+        def _():
+            halo(source).start()
+
+        @pl.when((source == 0) & (g > 1))
+        def _():
+            edge(0).start()
+
+        @pl.when((source == 7) & (g < gates - 1))
+        def _():
+            edge(1).start()
+
+    pass_on(me)
+
+    def arrive(k, carry):
+        source = lax.rem(me + k, 8)
+        block(me, source).wait_recv()
+        pass_on(source)
+        return carry
+
+    lax.fori_loop(1, 8, arrive, 0)
+
+    @pl.when(g < gates - 1)
+    def _():
+        for source in range(8):
+            halo(source).wait_recv()
+
+    @pl.when(g < gates - 2)
+    def _():
+        edge(0).wait_recv()
+
+    @pl.when(g > 0)
+    def _():
+        edge(1).wait_recv()
+
     compress(y_ref, taps_ref, sum_ref)
-    frame(first_ref[0] > 0, sum_ref, frame_ref)
+    frame(g == 0, sum_ref, frame_ref)
+
+    @pl.when(g > 0)
+    def _():
+        for source in range(8):
+            halo(source).wait_send()
+
+    @pl.when(g > 1)
+    def _():
+        edge(0).wait_send()
+
+    @pl.when(g < gates - 1)
+    def _():
+        edge(1).wait_send()
+
+    for k in range(1, 8):
+        weight(peer(k), me).wait_send()
+        block(peer(k), me).wait_send()
+
+    def sent(chunk, carry):
+        for k in range(1, 8):
+            strip(chunk, peer(k), me).wait_send()
+        return carry
+
+    lax.fori_loop(0, CHUNKS, sent, 0)
+
+
+def beams(echoes, weights, replica):
+    dft, cos, sin = tables()
+    dma = pltpu.SemaphoreType.DMA
+    return pl.pallas_call(
+        beams_kernel,
+        out_shape=jax.ShapeDtypeStruct((33 * UNITS * 8, 128), F32),
+        in_specs=[VMEM] * 6,
+        out_specs=VMEM,
+        scratch_shapes=[
+            pltpu.VMEM((CHUNKS, 8, 2, PER, 32, 256), BF16),
+            pltpu.VMEM((CHUNKS, 8, 2, PER, 32, 256), BF16),
+            pltpu.VMEM((8, 2, 32, 128), F32),
+            pltpu.VMEM((32, 256, 128), F32),
+            pltpu.VMEM((256, 512), BF16),
+            pltpu.VMEM((2, 2, 272, 256), F32),
+            pltpu.VMEM((8, 2, 2 * ROWS, 256), BF16),
+            pltpu.VMEM((34, 2 * ROWS, 256), BF16),
+            pltpu.VMEM((17, 256, 256), BF16),
+            pltpu.VMEM((UNITS * 2 * ROWS, 256), F32),
+            dma((CHUNKS, 8)),
+            dma((CHUNKS, 8)),
+            dma((CHUNKS,)),
+            dma((8,)),
+            dma((8,)),
+            dma((8,)),
+            dma((8,)),
+            dma((8,)),
+            dma((8,)),
+            dma((2,)),
+            dma((2,)),
+        ],
+        compiler_params=params(48, collective_id=0, has_side_effects=True),
+        cost_estimate=pl.CostEstimate(flops=6 * 10**9, bytes_accessed=8 << 20, transcendentals=0),
+    )(echoes, weights, replica, jnp.asarray(dft), jnp.asarray(cos), jnp.asarray(sin))
+
+
+def tiles_kernel(base_ref, shift_ref, slot_ref, frame_ref, out_ref, tile_ref):
     tile_ref[...] = jnp.zeros_like(tile_ref)
 
     def step(k, carry):
@@ -229,12 +507,6 @@
     slots = out_ref.shape[0]
     for k in range(8):
         out_ref[:, 128 * k : 128 * k + 128] = in_ref[pl.ds(k, slots, stride=8), :]
-
-
-def shifted(value, steps):
-    count = lax.axis_size("gate")
-    pairs = [(i, i + steps) for i in range(count) if 0 <= i + steps < count]
-    return lax.ppermute(value, "gate", pairs)
 
 
 def params(mib, **more):
@@ -246,34 +518,8 @@
     owners = pulse_devices * gate_devices
     tracks = track_owner.shape[0]
     capacity = 5
-    dft, cos, sin = tables()
-
-    strips = jnp.transpose(echoes, (3, 0, 1, 2)).reshape(8, 32, 2, 8, 256).transpose(0, 2, 3, 1, 4)
-    gathered = lax.all_to_all(strips, "pulse", split_axis=0, concat_axis=0, tiled=True)
-    weights = lax.all_gather(beam_weights, "pulse", axis=3, tiled=True).reshape(32, 16, 128)
-    taps = pl.pallas_call(
-        taps_kernel,
-        out_shape=jax.ShapeDtypeStruct((17, 256, 256), BF16),
-        in_specs=[VMEM],
-        out_specs=VMEM,
-        compiler_params=params(24),
-        cost_estimate=pl.CostEstimate(flops=10**7, bytes_accessed=2**22, transcendentals=0),
-    )(replica)
-
-    blocks = pl.pallas_call(
-        doppler_kernel,
-        out_shape=jax.ShapeDtypeStruct((8, 2, 2 * ROWS, 256), BF16),
-        in_specs=[VMEM] * 5,
-        out_specs=VMEM,
-        scratch_shapes=[pltpu.VMEM((256, 512), BF16), pltpu.VMEM((2, 2, 272, 256), F32)],
-        compiler_params=params(24),
-    )(gathered, weights, jnp.asarray(dft), jnp.asarray(cos), jnp.asarray(sin))
-    own = lax.all_to_all(blocks, "pulse", split_axis=0, concat_axis=0, tiled=True).reshape(
-        16, 2 * ROWS, 256
-    )
-    y = jnp.concatenate(
-        [shifted(own[15:], 1), own, shifted(own, -1), shifted(own[:1], -2)], axis=0
-    )
+    weights = beam_weights.reshape(32, 2, 128).transpose(1, 0, 2)
+    frames = beams(echoes, weights, replica)
 
     row_in, gate_in = track_doppler % 256, track_gate % 256 + 8
     base = row_in // 8 * UNITS + gate_in // 16
@@ -282,20 +528,15 @@
     earlier = (track_owner[:, None] == track_owner[None, :]) & (order[None, :] < order[:, None])
     rank = jnp.sum(earlier.astype(jnp.int32), axis=1, dtype=jnp.int32)
     slot = track_owner * capacity + rank
-    first = (lax.axis_index("gate") == 0).astype(jnp.int32).reshape(1)
 
     outgoing = pl.pallas_call(
         tiles_kernel,
         out_shape=jax.ShapeDtypeStruct((owners, capacity * 8, 128), BF16),
-        in_specs=[SMEM] * 4 + [VMEM] * 2,
+        in_specs=[SMEM] * 3 + [VMEM],
         out_specs=VMEM,
-        scratch_shapes=[
-            pltpu.VMEM((UNITS * 2 * ROWS, 256), F32),
-            pltpu.VMEM((33 * UNITS * 8, 128), F32),
-            pltpu.VMEM((owners * capacity, 8, 128), F32),
-        ],
-        compiler_params=params(32),
-    )(first, base, shift, slot, y, taps)
+        scratch_shapes=[pltpu.VMEM((owners * capacity, 8, 128), F32)],
+        compiler_params=params(24),
+    )(base, shift, slot, frames)
     received = lax.all_to_all(
         outgoing, ("pulse", "gate"), split_axis=0, concat_axis=0, tiled=True
     )

time: 142 us -> 102 us (0.72)
  blocking collectives: 90.5 us -> 32.5 us
  Pallas kernels: 16.9 us -> 62.1 us
  starting transfers between devices: 22.5 us -> 0 us
  waiting for transfers between devices: 5.46 us -> 0 us
    all_gather x1 -> x0, blocking collectives: 50.1 us -> none  [local(): lax.all_gather(beam_weights, 'pulse', axis=3, tiled=True)]
    pallas_call x2 -> x1, Pallas kernels: 6.83 us -> 56.1 us  [beams(): pl.pallas_call(beams_kernel, out_shape=jax.ShapeDtypeStruct((33 * UNITS *...]
    ppermute x3 -> x0, starting transfers between devices: 14.2 us -> none  [shifted(): return lax.ppermute(value, 'gate', pairs)]
    all_to_all x1 -> x0, blocking collectives: 12.3 us -> none  [local(): lax.all_to_all(blocks, 'pulse', split_axis=0, concat_axis=0, tiled=True)]
    all_to_all x1 -> x0, starting transfers between devices: 8.31 us -> none  [local(): lax.all_to_all(strips, 'pulse', split_axis=0, concat_axis=0, tiled=True)]
    ppermute x3 -> x0, waiting for transfers between devices: 5.46 us -> none  [shifted(): return lax.ppermute(value, 'gate', pairs)]
    all_to_all x1, blocking collectives: 28.1 us -> 32.5 us  [local(): lax.all_to_all(outgoing, ('pulse', 'gate'), split_axis=0, concat_axis=0,...]
    pallas_call x1, Pallas kernels: 7.94 us -> 3.89 us  [local(): pl.pallas_call(tiles_kernel, out_shape=jax.ShapeDtypeStruct((owners, capa...]
  transfers between devices with their start and end apart: 4 -> 0, of which waited for: 1 -> 0; matrix products, arithmetic and copies ran while one was open for 0% -> 0% of each run, Pallas kernels for 0% -> 0%
where the time goes in v2:
time: 102 us
  Pallas kernels  62.1 us (61%)
  blocking collectives  32.5 us (32%)
  local copies, waits for them, and re-layouts  5.49 us (5%)
  other arithmetic  1.92 us (2%)
    pallas_call x1, Pallas kernels, beams(): pl.pallas_call(beams_kernel, out_shape=jax.ShapeDtypeStruct((33 * UNITS *...  56.1 us
    all_to_all x1, blocking collectives, local(): lax.all_to_all(outgoing, ('pulse', 'gate'), split_axis=0, concat_axis=0,...  32.5 us
    unnamed x10, local copies, waits for them, and re-layouts  4.7 us
    pallas_call x1, Pallas kernels, local(): pl.pallas_call(tiles_kernel, out_shape=jax.ShapeDtypeStruct((owners, capa...  3.89 us
    pallas_call x1, Pallas kernels, local(): pl.pallas_call(rows_kernel, out_shape=jax.ShapeDtypeStruct((owners * capa...  2.09 us

profile of v2, /device:TPU:1, one launch (start us, length us, event | category | flops | bytes accessed | tf_op | source)
XLA Modules:
  0.0 102.0 jit_solution(6143418557728106050)
XLA Ops:
  0.0 0.9 convert_reduce_fusion
  0.9 0.8 reshape.8
  1.7 0.7 fusion.4
  2.5 0.0 copy-start
  2.5 1.6 %copy-done = bf16[2,8,256,256]{3,2,1,0:T(8,128)(2,1)S(1)} copy-done((bf16[2,8,256,256]{3,2,1,0:T(8,128)(2,1)S(1)}, bf16[2,8,256,256]{3,2,1,0:T(8,128)(2,1)}, u32[]{:S(2)}) %copy-start) | copy-done | bytes 2097176
  4.1 0.0 copy-start.1
  4.1 0.7 copy-done.1
  4.7 0.0 copy-start.2
  4.7 1.0 %copy-done.2 = bf16[512,512]{1,0:T(8,128)(2,1)S(1)} copy-done((bf16[512,512]{1,0:T(8,128)(2,1)S(1)}, bf16[512,512]{1,0:T(8,128)(2,1)}, u32[]{:S(2)}) %copy-start.2) | copy-done | bytes 524312
  5.8 0.0 copy-start.3
  5.8 0.7 copy-done.3
  6.5 0.0 copy-start.4
  6.5 0.7 copy-done.4
  7.2 56.1 %shard_map.91.frame_ref = f32[4752,128]{1,0:T(8,128)S(1)} custom-call(bf16[2,8,256,256]{3,2,1,0:T(8,128)(2,1)S(1)} %copy-done, f32[2,32,128]{2,1,0:T(8,128)S(1)} %bitcast.8, bf16[2,256]{1,0:T(2,128)(2,1)S(1)} %copy-done.1, bf16[512,512]{1,0:T(8,128)(2,1)S(1)} %copy-done.2, f32[8,256]{1,0:T(8,128)S(1)} %copy-done.4, f32[8,256]{1,0:T(8,128)S(1)} %copy-done.3), custom_call_target="tpu_custom_call" | custom-call | flops 6000000000 | bytes 8388608 | tf_op jit(solution)/shard_map/pallas_call | solution.py:462
  63.3 3.9 %shard_map.92 = bf16[128,40,128]{2,1,0:T(8,128)(2,1)S(1)} custom-call(s32[256]{0:T(256)S(1)} %get-tuple-element.6.base_ref, s32[256]{0:T(256)S(1)} %get-tuple-element.5.shift_ref, s32[256]{0:T(256)S(1)} %get-tuple-element.7.slot_ref, f32[4752,128]{1,0:T(8,128)S(1)} %shard_map.91.frame_ref), custom_call_target="tpu_custom_call" | custom-call | tf_op jit(solution)/shard_map/pallas_call | solution.py:532
  67.2 32.5 %all_to_all.5 = bf16[128,40,128]{2,1,0:T(8,128)(2,1)S(1)} all-to-all(bf16[128,40,128]{2,1,0:T(8,128)(2,1)S(1)} %shard_map.92), channel_id=1, replica_groups=mesh['pulse'=8,'gate'=16] {'pulse','gate'}, dimensions={0} | all-to-all | bytes 2621440 | tf_op jit(solution)/shard_map/all_to_all | solution.py:540
  99.7 0.3 bitcast_convert_fusion.in_ref
  99.9 2.1 %shard_map.93 = f32[640,1024]{1,0:T(8,128)} custom-call(f32[5120,128]{1,0:T(8,128)S(1)} %bitcast_convert_fusion.in_ref), custom_call_target="tpu_custom_call" | custom-call | tf_op jit(solution)/shard_map/pallas_call | solution.py:544
  (1 shorter events, 0.0 us)
Async XLA Ops:
  2.5 1.6 %copy-start = (bf16[2,8,256,256]{3,2,1,0:T(8,128)(2,1)S(1)}, bf16[2,8,256,256]{3,2,1,0:T(8,128)(2,1)}, u32[]{:S(2)}) copy-start(bf16[2,8,256,256]{3,2,1,0:T(8,128)(2,1)} %echo_ref.1) | copy-start | bytes 6291460
  4.1 0.7 copy-start.1
  4.7 1.0 %copy-start.2 = (bf16[512,512]{1,0:T(8,128)(2,1)S(1)}, bf16[512,512]{1,0:T(8,128)(2,1)}, u32[]{:S(2)}) copy-start(bf16[512,512]{1,0:T(8,128)(2,1)} %constant.77.clone.dft_ref) | copy-start | bytes 1572868
  5.8 0.7 copy-start.3
  6.5 0.7 copy-start.4

commit v3 on v2

--- a/solution.py
+++ b/solution.py
@@ -189,10 +189,7 @@
     gate = lane & 15
     gate_shift = shift & 15
     near_row, near_gate = lane >= shift - gate_shift, gate >= gate_shift
-    f = [
-        frame_ref[pl.ds(pl.multiple_of((base + step) * 8, 8), 8), :]
-        for step in (0, 1, UNITS, UNITS + 1)
-    ]
+    f = [frame_ref[base + step] for step in (0, 1, UNITS, UNITS + 1)]
     z = jnp.where(
         near_row, jnp.where(near_gate, f[0], f[1]), jnp.where(near_gate, f[2], f[3])
     )
@@ -208,13 +205,19 @@
 
 
 def beams_kernel(
-    echo_ref,
-    weight_ref,
+    echo_hbm,
+    weights_ref,
     replica_ref,
-    dft_ref,
+    dft_hbm,
     cos_ref,
     sin_ref,
+    codes_ref,
+    tiles_ref,
+    echo_ref,
+    dft_ref,
+    weight_ref,
     frame_ref,
+    out_tile,
     out_strip,
     in_strip,
     all_weights,
@@ -236,6 +239,11 @@
     halo_here,
     edge_sent,
     edge_here,
+    echo_loaded,
+    dft_loaded,
+    tile_sent,
+    tile_here,
+    row_here,
 ):
     me, g = lax.axis_index("pulse"), lax.axis_index("gate")
     gates = lax.axis_size("gate")
@@ -247,16 +255,22 @@
     def peer(k):
         return lax.rem(me + k, 8)
 
+    def load(chunk):
+        channels = pl.ds(chunk * PER, PER)
+        return pltpu.make_async_copy(
+            echo_hbm.at[:, channels], echo_ref.at[:, channels], echo_loaded.at[chunk]
+        )
+
+    def load_dft():
+        return pltpu.make_async_copy(dft_hbm, dft_ref, dft_loaded)
+
+    for chunk in range(CHUNKS):
+        load(chunk).start()
+    load_dft().start()
     for k in range(1, 8):
         pl.semaphore_signal(barrier, inc=1, **at(peer(k), g))
-    near = jnp.int32(7)
-    for step in (-2, -1, 1, 2):
-        there = (g + step >= 0) & (g + step < gates)
-        near += there.astype(jnp.int32)
-
-        @pl.when(there)
-        def _():
-            pl.semaphore_signal(barrier, inc=1, **at(me, g + step))
+    for k in range(1, gates):
+        pl.semaphore_signal(barrier, inc=1, **at(me, lax.rem(g + k, gates)))
 
     def strip(chunk, target, source):
         return pltpu.make_async_remote_copy(
@@ -309,6 +323,7 @@
         )
 
     def turn_chunk(chunk):
+        load(chunk).wait()
         for c in range(PER):
             for q in range(2):
                 turned = echo_ref[q, chunk * PER + c].T
@@ -319,9 +334,13 @@
             strip(chunk, peer(k), me).start()
         own_strip(chunk).start()
 
+    for half in range(2):
+        weight_ref[half] = weights_ref[:, 128 * half : 128 * half + 128]
     turn_chunk(0)
-    pl.semaphore_wait(barrier, near)
+    pl.semaphore_wait(barrier, 7 + gates - 1)
     send_chunk(0)
+    for k in range(1, 8):
+        pl.semaphore_signal(row_here, inc=1, **at(peer(k), g))
     for k in range(1, 8):
         weight(peer(k), me).start()
 
@@ -358,6 +377,8 @@
         return carry
 
     lax.fori_loop(0, 32, widen_step, 0)
+
+    load_dft().wait()
 
     def doppler_chunk(chunk, carry):
         own_strip(chunk).wait()
@@ -429,7 +450,37 @@
         edge(1).wait_recv()
 
     compress(y_ref, taps_ref, sum_ref)
-    frame(g == 0, sum_ref, frame_ref)
+    frame(g == 0, sum_ref, frame_ref.reshape(33 * UNITS * 8, 128))
+
+    pl.semaphore_wait(row_here, 7)
+    devices = 8 * gates
+    here = me * gates + g
+
+    def cut_block(owner):
+        tiles = []
+        for slot in range(5):
+            code = codes_ref[owner * 5 + slot]
+            tile = cut(lax.shift_right_logical(code, 8), code & 127, frame_ref)
+            tiles.append(jnp.where(code & 128 != 0, tile, 0.0))
+        return jnp.concatenate(tiles, axis=0).astype(BF16)
+
+    def tile(owner, holder):
+        return pltpu.make_async_remote_copy(
+            src_ref=out_tile.at[owner],
+            dst_ref=tiles_ref.at[holder],
+            send_sem=tile_sent,
+            recv_sem=tile_here,
+            **at(owner // gates, lax.rem(owner, gates)),
+        )
+
+    def cut_and_send(k, carry):
+        owner = lax.rem(here + k * 45, devices)
+        out_tile[owner] = cut_block(owner)
+        tile(owner, here).start()
+        return carry
+
+    lax.fori_loop(1, devices, cut_and_send, 0)
+    tiles_ref[here] = cut_block(here)
 
     @pl.when(g > 0)
     def _():
@@ -454,17 +505,32 @@
         return carry
 
     lax.fori_loop(0, CHUNKS, sent, 0)
-
-
-def beams(echoes, weights, replica):
+    everyone = pltpu.make_async_remote_copy(
+        src_ref=out_tile.at[pl.ds(0, devices - 1)],
+        dst_ref=tiles_ref.at[pl.ds(0, devices - 1)],
+        send_sem=tile_sent,
+        recv_sem=tile_here,
+        **at(me, g),
+    )
+    everyone.wait_recv()
+    everyone.wait_send()
+
+
+def tiles(echoes, weights, replica, codes, owners):
     dft, cos, sin = tables()
     dma = pltpu.SemaphoreType.DMA
+    hbm = pl.BlockSpec(memory_space=pltpu.HBM)
     return pl.pallas_call(
         beams_kernel,
-        out_shape=jax.ShapeDtypeStruct((33 * UNITS * 8, 128), F32),
-        in_specs=[VMEM] * 6,
+        out_shape=jax.ShapeDtypeStruct((owners, ROWS, 128), BF16),
+        in_specs=[hbm, VMEM, VMEM, hbm, VMEM, VMEM, SMEM],
         out_specs=VMEM,
         scratch_shapes=[
+            pltpu.VMEM((2, 8, 256, 256), BF16),
+            pltpu.VMEM((512, 512), BF16),
+            pltpu.VMEM((2, 32, 128), F32),
+            pltpu.VMEM((33 * UNITS, 8, 128), F32),
+            pltpu.VMEM((owners, ROWS, 128), BF16),
             pltpu.VMEM((CHUNKS, 8, 2, PER, 32, 256), BF16),
             pltpu.VMEM((CHUNKS, 8, 2, PER, 32, 256), BF16),
             pltpu.VMEM((8, 2, 32, 128), F32),
@@ -486,25 +552,20 @@
             dma((8,)),
             dma((2,)),
             dma((2,)),
+            dma((CHUNKS,)),
+            dma(()),
+            dma(()),
+            dma(()),
+            pltpu.SemaphoreType.REGULAR,
         ],
         compiler_params=params(48, collective_id=0, has_side_effects=True),
         cost_estimate=pl.CostEstimate(flops=6 * 10**9, bytes_accessed=8 << 20, transcendentals=0),
-    )(echoes, weights, replica, jnp.asarray(dft), jnp.asarray(cos), jnp.asarray(sin))
-
-
-def tiles_kernel(base_ref, shift_ref, slot_ref, frame_ref, out_ref, tile_ref):
-    tile_ref[...] = jnp.zeros_like(tile_ref)
-
-    def step(k, carry):
-        tile_ref[slot_ref[k]] = cut(base_ref[k], shift_ref[k], frame_ref)
-        return carry
-
-    lax.fori_loop(0, base_ref.shape[0], step, 0, unroll=8)
-    out_ref[...] = tile_ref[...].reshape(out_ref.shape).astype(BF16)
-
-
-def rows_kernel(in_ref, out_ref):
+    )(echoes, weights, replica, jnp.asarray(dft), jnp.asarray(cos), jnp.asarray(sin), codes)
+
+
+def rows_kernel(tiles_ref, out_ref, in_ref):
     slots = out_ref.shape[0]
+    in_ref[...] = tiles_ref[...].reshape(8 * slots, 128).astype(F32)
     for k in range(8):
         out_ref[:, 128 * k : 128 * k + 128] = in_ref[pl.ds(k, slots, stride=8), :]
 
@@ -518,9 +579,6 @@
     owners = pulse_devices * gate_devices
     tracks = track_owner.shape[0]
     capacity = 5
-    weights = beam_weights.reshape(32, 2, 128).transpose(1, 0, 2)
-    frames = beams(echoes, weights, replica)
-
     row_in, gate_in = track_doppler % 256, track_gate % 256 + 8
     base = row_in // 8 * UNITS + gate_in // 16
     shift = row_in % 8 * 16 + gate_in % 16
@@ -529,25 +587,18 @@
     rank = jnp.sum(earlier.astype(jnp.int32), axis=1, dtype=jnp.int32)
     slot = track_owner * capacity + rank
 
-    outgoing = pl.pallas_call(
-        tiles_kernel,
-        out_shape=jax.ShapeDtypeStruct((owners, capacity * 8, 128), BF16),
-        in_specs=[SMEM] * 3 + [VMEM],
-        out_specs=VMEM,
-        scratch_shapes=[pltpu.VMEM((owners * capacity, 8, 128), F32)],
-        compiler_params=params(24),
-    )(base, shift, slot, frames)
-    received = lax.all_to_all(
-        outgoing, ("pulse", "gate"), split_axis=0, concat_axis=0, tiled=True
-    )
-    wide = received.reshape(owners * capacity * 8, 128).astype(F32)
+    place = jnp.arange(owners * capacity, dtype=jnp.int32)
+    code = base * 256 + shift + 128
+    codes = jnp.sum(jnp.where(slot[None, :] == place[:, None], code[None, :], 0), axis=1, dtype=jnp.int32)
+    received = tiles(echoes, beam_weights.reshape(32, 256), replica, codes, owners)
     return pl.pallas_call(
         rows_kernel,
         out_shape=jax.ShapeDtypeStruct((owners * capacity, 1024), F32),
         in_specs=[VMEM],
         out_specs=VMEM,
+        scratch_shapes=[pltpu.VMEM((owners * capacity * 8, 128), F32)],
         compiler_params=params(16),
-    )(wide)
+    )(received)
 
 
 def solution(mesh):

time: 102 us -> 89.8 us (0.88)
  blocking collectives: 32.5 us -> 0 us
  Pallas kernels: 62.1 us -> 81.9 us
    all_to_all x1 -> x0, blocking collectives: 32.5 us -> none  [local(): lax.all_to_all(outgoing, ('pulse', 'gate'), split_axis=0, concat_axis=0,...]
    pallas_call x2 -> x1, Pallas kernels: 60 us -> 79.7 us  [tiles(): pl.pallas_call(beams_kernel, out_shape=jax.ShapeDtypeStruct((owners, ROWS...]
    unnamed x10 -> x12, local copies, waits for them, and re-layouts: 4.7 us -> 5.46 us
where the time goes in v3:
time: 89.8 us; the launch traced here: 89.2 us
  Pallas kernels  81.9 us (91%)
  local copies, waits for them, and re-layouts  5.46 us (6%)
  other arithmetic  1.85 us (2%)
    pallas_call x1, Pallas kernels, tiles(): pl.pallas_call(beams_kernel, out_shape=jax.ShapeDtypeStruct((owners, ROWS...  79.7 us
    unnamed x12, local copies, waits for them, and re-layouts  5.46 us
    pallas_call x1, Pallas kernels, local(): pl.pallas_call(rows_kernel, out_shape=jax.ShapeDtypeStruct((owners * capa...  2.25 us

profile of v3, /device:TPU:1, one launch (start us, length us, event | category | flops | bytes accessed | tf_op | source)
XLA Modules:
  0.0 89.2 jit_solution(8594653691162368894)
XLA Ops:
  0.0 0.9 %convert_reduce_fusion = s32[256]{0:T(256)S(1)} fusion(s32[256]{0:T(256)} %param.14), kind=kLoop, calls=%fused_computation.2 | loop fusion | flops 327424 | bytes 2048 | tf_op jit(solution)/shard_map/reduce_sum | solution.py:587
  0.9 0.7 multiply_add_fusion
  1.7 0.2 select_reduce_fusion.codes_ref
  1.9 0.0 copy-start
  1.9 1.6 %copy-done = bf16[2,8,256,256]{3,2,1,0:T(8,128)(2,1)S(1)} copy-done((bf16[2,8,256,256]{3,2,1,0:T(8,128)(2,1)S(1)}, bf16[2,8,256,256]{3,2,1,0:T(8,128)(2,1)}, u32[]{:S(2)}) %copy-start) | copy-done | bytes 2097176
  3.4 0.0 copy-start.1
  3.4 0.8 copy-done.1
  4.2 0.0 copy-start.2
  4.2 0.7 copy-done.2
  4.9 0.0 copy-start.3
  4.9 1.0 %copy-done.3 = bf16[512,512]{1,0:T(8,128)(2,1)S(1)} copy-done((bf16[512,512]{1,0:T(8,128)(2,1)S(1)}, bf16[512,512]{1,0:T(8,128)(2,1)}, u32[]{:S(2)}) %copy-start.3) | copy-done | bytes 524312
  5.9 0.0 copy-start.4
  5.9 0.7 copy-done.4
  6.6 0.0 copy-start.5
  6.6 0.7 copy-done.5
  7.3 79.7 %shard_map.91.tiles_ref = bf16[128,40,128]{2,1,0:T(8,128)(2,1)S(1)} custom-call(bf16[2,8,256,256]{3,2,1,0:T(8,128)(2,1)S(1)} %copy-done, f32[32,256]{1,0:T(8,128)S(1)} %bitcast.1, bf16[2,256]{1,0:T(2,128)(2,1)S(1)} %copy-done.2, bf16[512,512]{1,0:T(8,128)(2,1)S(1)} %copy-done.3, f32[8,256]{1,0:T(8,128)S(1)} %copy-done.5, f32[8,256]{1,0:T(8,128)S(1)} %copy-done.4, ...), custom_call_target="tpu_custom_call" | custom-call | flops 6000000000 | bytes 8388608 | tf_op jit(solution)/shard_map/pallas_call | solution.py:523
  87.0 2.2 %shard_map.92 = f32[640,1024]{1,0:T(8,128)} custom-call(bf16[128,40,128]{2,1,0:T(8,128)(2,1)S(1)} %shard_map.91.tiles_ref), custom_call_target="tpu_custom_call" | custom-call | tf_op jit(solution)/shard_map/pallas_call | solution.py:594
Async XLA Ops:
  1.9 1.6 %copy-start = (bf16[2,8,256,256]{3,2,1,0:T(8,128)(2,1)S(1)}, bf16[2,8,256,256]{3,2,1,0:T(8,128)(2,1)}, u32[]{:S(2)}) copy-start(bf16[2,8,256,256]{3,2,1,0:T(8,128)(2,1)} %echo_hbm.1) | copy-start | bytes 6291460
  3.4 0.8 copy-start.1
  4.2 0.7 copy-start.2
  4.9 1.0 %copy-start.3 = (bf16[512,512]{1,0:T(8,128)(2,1)S(1)}, bf16[512,512]{1,0:T(8,128)(2,1)}, u32[]{:S(2)}) copy-start(bf16[512,512]{1,0:T(8,128)(2,1)} %constant.80.clone.dft_hbm) | copy-start | bytes 1572868
  5.9 0.7 copy-start.4
  6.6 0.7 copy-start.5

commit v4 on v3

v4 whole, which is shorter than its diff:
```python
import functools
import math

import jax
import jax.numpy as jnp
import numpy as np
from jax import lax
from jax.experimental import pallas as pl
from jax.experimental.pallas import tpu as pltpu
from jax.sharding import PartitionSpec as P

F32 = jnp.float32
BF16 = jnp.bfloat16
UNITS = 18
ROWS = 40
VMEM = pl.BlockSpec(memory_space=pltpu.VMEM)
SMEM = pl.BlockSpec(memory_space=pltpu.SMEM)


def tables():
    angle = 2.0 * np.pi * ((np.arange(256)[:, None] * np.arange(256)[None, :]) % 256) / 256.0
    cos, sin = np.cos(angle), np.sin(angle)
    dft = np.block([[cos, sin], [-sin, cos]]).astype(jnp.bfloat16)
    twist = 2.0 * np.pi * (np.arange(8)[:, None] * np.arange(256)[None, :]) / 2048.0
    scale = 1.0 / 1024.0
    return dft, np.stack([np.cos(twist) * scale, np.sin(twist) * scale]).astype(np.float32)


def cadd(a, b):
    return (a[0] + b[0], a[1] + b[1])


def csub(a, b):
    return (a[0] - b[0], a[1] - b[1])


def turn(a):
    return (a[1], -a[0])


def dft4(a):
    e0, e1 = cadd(a[0], a[2]), csub(a[0], a[2])
    f0, f1 = cadd(a[1], a[3]), turn(csub(a[1], a[3]))
    return [cadd(e0, f0), cadd(e1, f1), csub(e0, f0), csub(e1, f1)]


def dft8(x):
    root = math.sqrt(0.5)
    even = dft4([cadd(x[k], x[k + 4]) for k in range(4)])
    b = [csub(x[k], x[k + 4]) for k in range(4)]
    b1 = ((b[1][0] + b[1][1]) * root, (b[1][1] - b[1][0]) * root)
    b3 = ((b[3][1] - b[3][0]) * root, (b[3][0] + b[3][1]) * -root)
    odd = dft4([b[0], b1, turn(b[2]), b3])
    return [(even, odd)[d % 2][d // 2] for d in range(8)]


def doppler_pair(pair, x_ref, wide_ref, dft_ref, twist_ref, z_ref, acc_ref):
    for c in range(2):
        for half in range(2):
            cols = slice(128 * half, 128 * half + 128)
            x = [tuple(x_ref[pb, q, c, :, cols].astype(F32) for q in range(2)) for pb in range(8)]
            for d, (re, im) in enumerate(dft8(x)):
                cos, sin = (twist_ref[k, d : d + 1, cols] for k in range(2))
                at = slice(128 * c + 16 * d, 128 * c + 16 * d + 16)
                z_ref[at, 128 * half : 128 * half + 128] = (re * cos + im * sin).astype(BF16)
                z_ref[at, 256 + 128 * half : 384 + 128 * half] = (im * cos - re * sin).astype(BF16)
    spec = lax.dot_general(
        dft_ref[...], z_ref[...], (((1,), (1,)), ((), ())), preferred_element_type=F32
    )
    for b in range(2):
        real, imag = 0.0, 0.0
        for c in range(2):
            w_re, w_im = (wide_ref[(q * 2 + b) * 8 + 2 * pair + c] for q in range(2))
            cols = slice(128 * c, 128 * c + 128)
            re, im = spec[:256, cols], spec[256:, cols]
            real += w_re * re - w_im * im
            imag += w_re * im + w_im * re
        acc_ref[0, b, 8:264] += real
        acc_ref[1, b, 8:264] += imag


def widen(i, weight_ref, wide_ref):
    lane = lax.broadcasted_iota(jnp.int32, (16, 128), 1)
    keep = lane // 8 == lax.broadcasted_iota(jnp.int32, (16, 128), 0)
    spread = (
        lax.broadcasted_iota(jnp.int32, (128, 128), 0) % 8
        == lax.broadcasted_iota(jnp.int32, (128, 128), 1) // 16
    )
    spread = jnp.where(spread, 1.0, 0.0).astype(BF16)
    w = jnp.concatenate(
        [
            jnp.where(keep, weight_ref[source, half, pl.ds(i, 1), :], 0.0)
            for source in range(8)
            for half in range(2)
        ],
        axis=0,
    )
    high = w.astype(BF16)
    rest = w - high.astype(F32)
    mid = rest.astype(BF16)
    low = (rest - mid.astype(F32)).astype(BF16)
    wide_ref[i] = sum(jnp.dot(part, spread, preferred_element_type=F32) for part in (low, mid, high))


def pack_block(j, acc_ref, out_ref):
    for q in range(2):
        both = jnp.concatenate(
            [acc_ref[q, b, 32 * j + 7 : 32 * j + 7 + ROWS] for b in range(2)], axis=0
        )
        out_ref[:, 128 * q : 128 * q + 128] = both.astype(BF16)


def make_taps(replica_ref, taps_ref):
    period = (
        lax.broadcasted_iota(jnp.int32, (16, 128), 0)
        == lax.broadcasted_iota(jnp.int32, (16, 128), 1) % 16
    )
    period = jnp.where(period, 1.0, 0.0).astype(F32)
    tables = []
    for q in range(2):
        row = jnp.concatenate(
            [replica_ref[q : q + 1, :].astype(F32), jnp.zeros((1, 128), F32)], axis=1
        )
        shifted = pltpu.roll(jnp.broadcast_to(row, (16, 384)), 0, 1, stride=1, stride_axis=0)
        tables.append(
            lax.dot_general(
                shifted.astype(BF16),
                period.astype(BF16),
                (((0,), (0,)), ((), ())),
                preferred_element_type=F32,
            )
        )
    lane = lax.broadcasted_iota(jnp.int32, (16, 128), 1) // 16
    for j in range(17):
        real, imag = (t[16 * j : 16 * j + 16] for t in tables)
        for d in range(8):
            keep = lane == d
            re, im = jnp.where(keep, real, 0.0), jnp.where(keep, imag, 0.0)
            from_real = jnp.concatenate([re, -im], axis=1).astype(BF16)
            from_imag = jnp.concatenate([im, re], axis=1).astype(BF16)
            taps_ref[j, 16 * d : 16 * d + 16, :] = from_real
            taps_ref[j, 128 + 16 * d : 144 + 16 * d, :] = from_imag


def compress(parity, y_ref, taps_ref, sum_ref):
    half, depth = UNITS // 2, 2 * ROWS
    for out in range(2):
        odd = (parity - out) % 2
        skip = out * (1 - parity)
        total = 9 - odd

        def part(first, count):
            x = jnp.concatenate(
                [
                    y_ref[parity, pl.ds(skip + first + k, half)].reshape(half * depth, 256)
                    for k in range(count)
                ],
                axis=1,
            )
            w = jnp.concatenate([taps_ref[odd + 2 * (first + k)] for k in range(count)], axis=0)
            return jnp.dot(x, w, preferred_element_type=F32)

        for first in range(0, 8, 4):
            count = 5 if first == 4 and total == 9 else 4
            if parity == 1 and first == 0:
                sum_ref[out] = part(first, count)
            else:
                sum_ref[out] += part(first, count)


def frame(first_block, sum_ref, frame_ref):
    for unit in range(UNITS):
        for q in range(2):
            for b in range(2):
                for half in range(2):
                    start = (unit // 2 * 2 + b) * ROWS + half
                    value = sum_ref[unit % 2, start : start + 33, 128 * q : 128 * q + 128]
                    if unit == 0:
                        value = jnp.where(first_block, 0.0, value)
                    at = pl.ds(unit * 8 + q * 4 + b * 2 + half, 33, stride=8 * UNITS)
                    frame_ref[at, :] = value


def slot_codes(doppler, gate, owner, slots):
    row, col = doppler & 255, (gate & 255) + 8
    base = lax.shift_right_logical(row, 3) * UNITS + lax.shift_right_logical(col, 4)
    code = (base * 256 + 128 + (row & 7) * 16 + (col & 15)).astype(F32)
    owner = owner.astype(F32)
    tracks = owner.shape[1]
    column = jnp.broadcast_to(owner, (8, tracks)).T[:, :1]
    square = (tracks, tracks)
    before = lax.broadcasted_iota(jnp.int32, square, 0) < lax.broadcasted_iota(jnp.int32, square, 1)
    same = jnp.where((column == owner) & before, 1.0, 0.0)
    slot = owner * 5.0 + jnp.sum(same, axis=0, keepdims=True)
    both = jnp.concatenate([slot, code, jnp.zeros((6, tracks), F32)], axis=0).T
    place = lax.broadcasted_iota(jnp.int32, (tracks, slots), 1).astype(F32)
    found = jnp.where(both[:, :1] == place, both[:, 1:2], 0.0)
    return jnp.sum(found, axis=0, keepdims=True).astype(jnp.int32)


def cut(base, shift, frame_ref):
    lane = lax.broadcasted_iota(jnp.int32, (8, 128), 1)
    gate = lane & 15
    gate_shift = shift & 15
    near_row, near_gate = lane >= shift - gate_shift, gate >= gate_shift
    f = [frame_ref[base + step] for step in (0, 1, UNITS, UNITS + 1)]
    z = jnp.where(
        near_row, jnp.where(near_gate, f[0], f[1]), jnp.where(near_gate, f[2], f[3])
    )
    return jnp.where(
        gate < 16 - gate_shift,
        pltpu.roll(z, (128 - shift) & 127, 1),
        pltpu.roll(z, (144 - shift) & 127, 1),
    )


PAIRS = 4


def tiles_kernel(
    echo_hbm,
    weights_hbm,
    replica_hbm,
    dft_hbm,
    twist_hbm,
    doppler_hbm,
    gate_hbm,
    owner_hbm,
    tiles_ref,
    echo_ref,
    weights_ref,
    replica_ref,
    dft_ref,
    twist_ref,
    track_ref,
    code_ref,
    codes_ref,
    weight_ref,
    frame_ref,
    out_tile,
    out_strip,
    in_strip,
    all_weights,
    wide_ref,
    z_ref,
    acc_ref,
    out_block,
    y_ref,
    taps_ref,
    sum_ref,
    strip_sent,
    strip_here,
    strip_own,
    weight_sent,
    weight_here,
    block_sent,
    block_here,
    halo_sent,
    halo_here,
    edge_sent,
    edge_here,
    echo_loaded,
    loaded,
    code_moved,
    tile_sent,
    tile_here,
    row_here,
):
    me, g = lax.axis_index("pulse"), lax.axis_index("gate")
    gates = lax.axis_size("gate")
    barrier = pltpu.get_barrier_semaphore()

    def at(pulse, gate):
        return dict(device_id=(pulse, gate), device_id_type=pl.DeviceIdType.MESH)

    def peer(k):
        return lax.rem(me + k, 8)

    def load(pair):
        channels = pl.ds(pair * 2, 2)
        return pltpu.make_async_copy(
            echo_hbm.at[:, channels], echo_ref.at[:, channels], echo_loaded.at[pair]
        )

    small = [
        (weights_hbm, weights_ref),
        (replica_hbm, replica_ref),
        (dft_hbm, dft_ref),
        (twist_hbm, twist_ref),
        (doppler_hbm, track_ref.at[0]),
        (gate_hbm, track_ref.at[1]),
        (owner_hbm, track_ref.at[2]),
    ]
    loads = [
        pltpu.make_async_copy(source, target, loaded.at[k])
        for k, (source, target) in enumerate(small)
    ]
    for k in range(1, 8):
        pl.semaphore_signal(barrier, inc=1, **at(peer(k), g))
    for k in range(1, gates):
        pl.semaphore_signal(barrier, inc=1, **at(me, lax.rem(g + k, gates)))
    for pair in range(PAIRS):
        load(pair).start()
    for copy in loads:
        copy.start()

    def strip(unit, pair, target, source):
        return pltpu.make_async_remote_copy(
            src_ref=out_strip.at[unit, pair, target],
            dst_ref=in_strip.at[unit, pair, source],
            send_sem=strip_sent.at[unit, pair, target],
            recv_sem=strip_here.at[unit, pair, source],
            **at(target, g),
        )

    def own_strip(unit, pair):
        return pltpu.make_async_copy(
            out_strip.at[unit, pair, me], in_strip.at[unit, pair, me], strip_own.at[unit, pair]
        )

    def weight(target, source):
        return pltpu.make_async_remote_copy(
            src_ref=weight_ref,
            dst_ref=all_weights.at[source],
            send_sem=weight_sent.at[target],
            recv_sem=weight_here.at[source],
            **at(target, g),
        )

    def block(u, target, source):
        return pltpu.make_async_remote_copy(
            src_ref=out_block.at[u, target],
            dst_ref=y_ref.at[1 - u, source + u],
            send_sem=block_sent.at[u, target],
            recv_sem=block_here.at[u, source],
            **at(target, g),
        )

    def halo(u, source):
        return pltpu.make_async_remote_copy(
            src_ref=y_ref.at[1 - u, source + u],
            dst_ref=y_ref.at[1 - u, source + u + 8],
            send_sem=halo_sent.at[u, source],
            recv_sem=halo_here.at[u, source],
            **at(me, g - 1),
        )

    def edge(u):
        return pltpu.make_async_remote_copy(
            src_ref=y_ref.at[1 - u, (0, 8)[u]],
            dst_ref=y_ref.at[1 - u, (16, 0)[u]],
            send_sem=edge_sent.at[u],
            recv_sem=edge_here.at[u],
            **at(me, (g - 2, g + 1)[u]),
        )

    def turn(pair):
        load(pair).wait()
        for c in range(2):
            for q in range(2):
                turned = echo_ref[q, pair * 2 + c].T.reshape(8, 2, 16, 256)
                for unit in range(2):
                    out_strip[unit, pair, :, q, c] = turned[:, unit]

    def send(unit, pair):
        for k in range(1, 8):
            strip(unit, pair, peer(k), me).start()
        own_strip(unit, pair).start()

    loads[0].wait()
    for half in range(2):
        weight_ref[half] = weights_ref[:, 128 * half : 128 * half + 128]
    turn(0)
    pl.semaphore_wait(barrier, 7 + gates - 1)
    for k in range(1, 8):
        weight(peer(k), me).start()
    send(0, 0)
    for k in range(1, 8):
        pl.semaphore_signal(row_here, inc=1, **at(peer(k), g))

    def turn_and_send(pair, carry):
        turn(pair)
        send(0, pair)
        return carry

    def send_second(pair, carry):
        send(1, pair)
        return carry

    lax.fori_loop(1, PAIRS, turn_and_send, 0)
    lax.fori_loop(0, PAIRS, send_second, 0)

    for copy in loads[1:]:
        copy.wait()
    code_ref[...] = slot_codes(track_ref[0], track_ref[1], track_ref[2], code_ref.shape[1])
    move = pltpu.make_async_copy(code_ref, codes_ref, code_moved)
    move.start()
    all_weights[me] = weight_ref[...]
    nothing = jnp.zeros((2 * ROWS, 256), BF16)

    @pl.when(g == 0)
    def _():
        y_ref[0, 0] = nothing

    @pl.when(g == gates - 1)
    def _():
        for k in range(8):
            y_ref[1, 8 + k] = nothing
            y_ref[0, 9 + k] = nothing

    @pl.when(g >= gates - 2)
    def _():
        y_ref[1, 16] = nothing

    make_taps(replica_ref, taps_ref)
    for k in range(1, 8):
        weight(me, peer(k)).wait_recv()

    def widen_step(i, carry):
        widen(i, all_weights, wide_ref)
        return carry

    lax.fori_loop(0, 32, widen_step, 0)
    move.wait()

    for u in range(2):
        acc_ref[...] = jnp.zeros_like(acc_ref)

        def transform(pair, carry):
            own_strip(u, pair).wait()
            for k in range(1, 8):
                strip(u, pair, me, peer(k)).wait_recv()
            doppler_pair(
                pair, in_strip.at[u, pair], wide_ref, dft_ref, twist_ref, z_ref, acc_ref
            )
            return carry

        lax.fori_loop(0, PAIRS, transform, 0)

        for j in range(8):

            @pl.when(me == j)
            def _():
                pack_block(j, acc_ref, y_ref.at[1 - u, j + u])

            @pl.when(me != j)
            def _():
                pack_block(j, acc_ref, out_block.at[u, j])
                block(u, j, me).start()

    def pass_on(u, source):
        @pl.when(g > 0)
        def _():
            halo(u, source).start()

        if u == 0:

            @pl.when((source == 0) & (g > 1))
            def _():
                edge(0).start()

        else:

            @pl.when((source == 7) & (g < gates - 1))
            def _():
                edge(1).start()

    for u in range(2):
        pass_on(u, me)

        def arrive(k, carry):
            source = peer(k)
            block(u, me, source).wait_recv()
            pass_on(u, source)
            return carry

        lax.fori_loop(1, 8, arrive, 0)

    for u in range(2):

        @pl.when(g < gates - 1)
        def _():
            for source in range(8):
                halo(u, source).wait_recv()

        @pl.when((g < gates - 2, g > 0)[u])
        def _():
            edge(u).wait_recv()

        compress(1 - u, y_ref, taps_ref, sum_ref)

    frame(g == 0, sum_ref, frame_ref.reshape(33 * UNITS * 8, 128))

    pl.semaphore_wait(row_here, 7)
    devices = 8 * gates
    here = me * gates + g

    def cut_block(owner):
        tiles = []
        for slot in range(5):
            code = codes_ref[0, owner * 5 + slot]
            base = jnp.clip(lax.shift_right_logical(code, 8), 0, 32 * UNITS - 2)
            tile = cut(base, code & 127, frame_ref)
            tiles.append(jnp.where(code & 128 != 0, tile, 0.0))
        return jnp.concatenate(tiles, axis=0).astype(BF16)

    def tile(owner, holder):
        return pltpu.make_async_remote_copy(
            src_ref=out_tile.at[owner],
            dst_ref=tiles_ref.at[holder],
            send_sem=tile_sent,
            recv_sem=tile_here,
            **at(owner // gates, lax.rem(owner, gates)),
        )

    def cut_and_send(k, carry):
        owner = lax.rem(here + k * 45, devices)
        out_tile[owner] = cut_block(owner)
        tile(owner, here).start()
        return carry

    lax.fori_loop(1, devices, cut_and_send, 0)
    tiles_ref[here] = cut_block(here)

    for u in range(2):

        @pl.when(g > 0)
        def _():
            for source in range(8):
                halo(u, source).wait_send()

        @pl.when((g > 1, g < gates - 1)[u])
        def _():
            edge(u).wait_send()

    for k in range(1, 8):
        weight(peer(k), me).wait_send()
        for u in range(2):
            block(u, peer(k), me).wait_send()

    def sent(pair, carry):
        for k in range(1, 8):
            for u in range(2):
                strip(u, pair, peer(k), me).wait_send()
        return carry

    lax.fori_loop(0, PAIRS, sent, 0)
    everyone = pltpu.make_async_remote_copy(
        src_ref=out_tile.at[pl.ds(0, devices - 1)],
        dst_ref=tiles_ref.at[pl.ds(0, devices - 1)],
        send_sem=tile_sent,
        recv_sem=tile_here,
        **at(me, g),
    )
    everyone.wait_recv()
    everyone.wait_send()


def tiles(echoes, weights, replica, doppler, gate, owner, owners):
    dft, twist = tables()
    dma = pltpu.SemaphoreType.DMA
    hbm = pl.BlockSpec(memory_space=pltpu.HBM)
    return pl.pallas_call(
        tiles_kernel,
        out_shape=jax.ShapeDtypeStruct((owners, ROWS, 128), BF16),
        in_specs=[hbm] * 8,
        out_specs=VMEM,
        scratch_shapes=[
            pltpu.VMEM((2, 8, 256, 256), BF16),
            pltpu.VMEM((32, 256), F32),
            pltpu.VMEM((2, 256), BF16),
            pltpu.VMEM((512, 512), BF16),
            pltpu.VMEM((2, 8, 256), F32),
            pltpu.VMEM((3, 1, 256), jnp.int32),
            pltpu.VMEM((1, owners * 5), jnp.int32),
            pltpu.SMEM((1, owners * 5), jnp.int32),
            pltpu.VMEM((2, 32, 128), F32),
            pltpu.VMEM((33 * UNITS, 8, 128), F32),
            pltpu.VMEM((owners, ROWS, 128), BF16),
            pltpu.VMEM((2, PAIRS, 8, 2, 2, 16, 256), BF16),
            pltpu.VMEM((2, PAIRS, 8, 2, 2, 16, 256), BF16),
            pltpu.VMEM((8, 2, 32, 128), F32),
            pltpu.VMEM((32, 256, 128), F32),
            pltpu.VMEM((256, 512), BF16),
            pltpu.VMEM((2, 2, 272, 128), F32),
            pltpu.VMEM((2, 8, 2 * ROWS, 256), BF16),
            pltpu.VMEM((2, 17, 2 * ROWS, 256), BF16),
            pltpu.VMEM((17, 256, 256), BF16),
            pltpu.VMEM((2, UNITS * ROWS, 256), F32),
            dma((2, PAIRS, 8)),
            dma((2, PAIRS, 8)),
            dma((2, PAIRS)),
            dma((8,)),
            dma((8,)),
            dma((2, 8)),
            dma((2, 8)),
            dma((2, 8)),
            dma((2, 8)),
            dma((2,)),
            dma((2,)),
            dma((PAIRS,)),
            dma((7,)),
            dma(()),
            dma(()),
            dma(()),
            pltpu.SemaphoreType.REGULAR,
        ],
        compiler_params=params(60, collective_id=0, has_side_effects=True),
        cost_estimate=pl.CostEstimate(flops=6 * 10**9, bytes_accessed=8 << 20, transcendentals=0),
    )(echoes, weights, replica, jnp.asarray(dft), jnp.asarray(twist), doppler, gate, owner)


def rows_kernel(tiles_ref, out_ref, in_ref):
    slots = out_ref.shape[0]
    in_ref[...] = tiles_ref[...].reshape(8 * slots, 128).astype(F32)
    for k in range(8):
        out_ref[:, 128 * k : 128 * k + 128] = in_ref[pl.ds(k, slots, stride=8), :]


def params(mib, **more):
    return pltpu.CompilerParams(vmem_limit_bytes=mib << 20, **more)


def local(echoes, replica, beam_weights, track_doppler, track_gate, track_owner):
    pulse_devices, gate_devices = lax.axis_size("pulse"), lax.axis_size("gate")
    owners = pulse_devices * gate_devices
    tracks = track_owner.shape[0]
    capacity = 5
    rows = (x.reshape(1, tracks) for x in (track_doppler, track_gate, track_owner))
    received = tiles(echoes, beam_weights.reshape(32, 256), replica, *rows, owners)
    return pl.pallas_call(
        rows_kernel,
        out_shape=jax.ShapeDtypeStruct((owners * capacity, 1024), F32),
        in_specs=[VMEM],
        out_specs=VMEM,
        scratch_shapes=[pltpu.VMEM((owners * capacity * 8, 128), F32)],
        compiler_params=params(16),
    )(received)


def solution(mesh):
    return jax.shard_map(
        local,
        mesh=mesh,
        in_specs=(
            P(None, None, "pulse", "gate"),
            P(),
            P(None, None, None, "pulse"),
            P(("pulse", "gate")),
            P(("pulse", "gate")),
            P(("pulse", "gate")),
        ),
        out_specs=P(("pulse", "gate"), None),
        check_vma=False,
    )
```

time: 89.8 us -> 92.5 us (1.030)
  the two profiles are of different devices: /device:TPU:1 before, /device:TPU:25 now
where the time goes in v4:
time: 92.5 us; the launch traced here: 92.3 us
  Pallas kernels  91 us (98%)
  local copies, waits for them, and re-layouts  1.31 us (1%)
    pallas_call x1, Pallas kernels, tiles(): pl.pallas_call(tiles_kernel, out_shape=jax.ShapeDtypeStruct((owners, ROWS...  88.8 us
    pallas_call x1, Pallas kernels, local(): pl.pallas_call(rows_kernel, out_shape=jax.ShapeDtypeStruct((owners * capa...  2.25 us

profile of v4, /device:TPU:25, one launch (start us, length us, event | category | flops | bytes accessed | tf_op | source)
XLA Modules:
  0.0 92.3 jit_solution(1301386210807222134)
XLA Ops:
  0.0 88.8 %shard_map.82.tiles_ref = bf16[128,40,128]{2,1,0:T(8,128)(2,1)} custom-call(bf16[2,8,256,256]{3,2,1,0:T(8,128)(2,1)} %echo_hbm.1, f32[32,256]{1,0:T(8,128)} %bitcast.4, bf16[2,256]{1,0:T(2,128)(2,1)} %replica_hbm.1, bf16[512,512]{1,0:T(8,128)(2,1)} %constant.4.clone.dft_hbm, f32[2,8,256]{2,1,0:T(8,128)} %constant.5.clone.twist_hbm, s32[1,256]{1,0:T(1,128)} %bitcast.5, ...), custom_call_target="tpu_custom_call" | custom-call | flops 6000000000 | bytes 8388608 | tf_op jit(solution)/shard_map/pallas_call | solution.py:563
  88.8 0.0 copy-start
  88.8 1.3 %copy-done = bf16[128,40,128]{2,1,0:T(8,128)(2,1)S(1)} copy-done((bf16[128,40,128]{2,1,0:T(8,128)(2,1)S(1)}, bf16[128,40,128]{2,1,0:T(8,128)(2,1)}, u32[]{:S(2)}) %copy-start) | copy-done | bytes 1310744
  90.1 2.2 %shard_map.83 = f32[640,1024]{1,0:T(8,128)} custom-call(bf16[128,40,128]{2,1,0:T(8,128)(2,1)S(1)} %copy-done), custom_call_target="tpu_custom_call" | custom-call | tf_op jit(solution)/shard_map/pallas_call | solution.py:631
Async XLA Ops:
  88.8 1.3 %copy-start = (bf16[128,40,128]{2,1,0:T(8,128)(2,1)S(1)}, bf16[128,40,128]{2,1,0:T(8,128)(2,1)}, u32[]{:S(2)}) copy-start(bf16[128,40,128]{2,1,0:T(8,128)(2,1)} %shard_map.82.tiles_ref) | copy-start | bytes 3932164

commit v5 on v4

--- a/solution.py
+++ b/solution.py
@@ -215,6 +215,8 @@
 
 
 PAIRS = 4
+EARLY = 4
+STEP = 3
 
 
 def tiles_kernel(
@@ -388,7 +390,7 @@
         return carry
 
     lax.fori_loop(1, PAIRS, turn_and_send, 0)
-    lax.fori_loop(0, PAIRS, send_second, 0)
+    lax.fori_loop(0, EARLY, send_second, 0)
 
     for copy in loads[1:]:
         copy.wait()
@@ -423,10 +425,8 @@
     lax.fori_loop(0, 32, widen_step, 0)
     move.wait()
 
-    for u in range(2):
-        acc_ref[...] = jnp.zeros_like(acc_ref)
-
-        def transform(pair, carry):
+    def transform(u, first, last):
+        def one(pair, carry):
             own_strip(u, pair).wait()
             for k in range(1, 8):
                 strip(u, pair, me, peer(k)).wait_recv()
@@ -435,8 +435,9 @@
             )
             return carry
 
-        lax.fori_loop(0, PAIRS, transform, 0)
-
+        lax.fori_loop(first, last, one, 0)
+
+    def send_blocks(u):
         for j in range(8):
 
             @pl.when(me == j)
@@ -465,7 +466,7 @@
             def _():
                 edge(1).start()
 
-    for u in range(2):
+    def pass_all(u):
         pass_on(u, me)
 
         def arrive(k, carry):
@@ -476,8 +477,7 @@
 
         lax.fori_loop(1, 8, arrive, 0)
 
-    for u in range(2):
-
+    def compress_unit(u):
         @pl.when(g < gates - 1)
         def _():
             for source in range(8):
@@ -489,6 +489,16 @@
 
         compress(1 - u, y_ref, taps_ref, sum_ref)
 
+    acc_ref[...] = jnp.zeros_like(acc_ref)
+    transform(0, 0, PAIRS)
+    send_blocks(0)
+    acc_ref[...] = jnp.zeros_like(acc_ref)
+    transform(1, 0, PAIRS)
+    send_blocks(1)
+    pass_all(0)
+    pass_all(1)
+    compress_unit(0)
+    compress_unit(1)
     frame(g == 0, sum_ref, frame_ref.reshape(33 * UNITS * 8, 128))
 
     pl.semaphore_wait(row_here, 7)
@@ -513,13 +523,20 @@
             **at(owner // gates, lax.rem(owner, gates)),
         )
 
-    def cut_and_send(k, carry):
-        owner = lax.rem(here + k * 45, devices)
+    def cut_and_send(step, carry):
+        near = [lax.rem(here + 1 + step * STEP + k, devices) for k in range(STEP)]
+        for owner, part in zip(near, [cut_block(owner) for owner in near]):
+            out_tile[owner] = part
+        for owner in near:
+            tile(owner, here).start()
+        return carry
+
+    steps = (devices - 1) // STEP
+    lax.fori_loop(0, steps, cut_and_send, 0)
+    for k in range(1 + steps * STEP, devices):
+        owner = lax.rem(here + k, devices)
         out_tile[owner] = cut_block(owner)
         tile(owner, here).start()
-        return carry
-
-    lax.fori_loop(1, devices, cut_and_send, 0)
     tiles_ref[here] = cut_block(here)
 
     for u in range(2):

time: 92.5 us -> 82.8 us (0.90)
  the two profiles are of different devices: /device:TPU:25 before, /device:TPU:1 now
where the time goes in v5:
time: 82.8 us; the launch traced here: 81.4 us
  Pallas kernels  80 us (97%)
  local copies, waits for them, and re-layouts  1.31 us (2%)
    pallas_call x1, Pallas kernels, tiles(): pl.pallas_call(tiles_kernel, out_shape=jax.ShapeDtypeStruct((owners, ROWS...  77.8 us
    pallas_call x1, Pallas kernels, local(): pl.pallas_call(rows_kernel, out_shape=jax.ShapeDtypeStruct((owners * capa...  2.25 us

profile of v5, /device:TPU:1, one launch (start us, length us, event | category | flops | bytes accessed | tf_op | source)
XLA Modules:
  0.0 81.4 jit_solution(10910730288743994030)
XLA Ops:
  0.0 77.8 %shard_map.82.tiles_ref = bf16[128,40,128]{2,1,0:T(8,128)(2,1)} custom-call(bf16[2,8,256,256]{3,2,1,0:T(8,128)(2,1)} %echo_hbm.1, f32[32,256]{1,0:T(8,128)} %bitcast.4, bf16[2,256]{1,0:T(2,128)(2,1)} %replica_hbm.1, bf16[512,512]{1,0:T(8,128)(2,1)} %constant.4.clone.dft_hbm, f32[2,8,256]{2,1,0:T(8,128)} %constant.5.clone.twist_hbm, s32[1,256]{1,0:T(1,128)} %bitcast.5, ...), custom_call_target="tpu_custom_call" | custom-call | flops 6000000000 | bytes 8388608 | tf_op jit(solution)/shard_map/pallas_call | solution.py:580
  77.8 0.0 copy-start
  77.8 1.3 %copy-done = bf16[128,40,128]{2,1,0:T(8,128)(2,1)S(1)} copy-done((bf16[128,40,128]{2,1,0:T(8,128)(2,1)S(1)}, bf16[128,40,128]{2,1,0:T(8,128)(2,1)}, u32[]{:S(2)}) %copy-start) | copy-done | bytes 1310744
  79.1 2.2 %shard_map.83 = f32[640,1024]{1,0:T(8,128)} custom-call(bf16[128,40,128]{2,1,0:T(8,128)(2,1)S(1)} %copy-done), custom_call_target="tpu_custom_call" | custom-call | tf_op jit(solution)/shard_map/pallas_call | solution.py:648
Async XLA Ops:
  77.8 1.3 %copy-start = (bf16[128,40,128]{2,1,0:T(8,128)(2,1)S(1)}, bf16[128,40,128]{2,1,0:T(8,128)(2,1)}, u32[]{:S(2)}) copy-start(bf16[128,40,128]{2,1,0:T(8,128)(2,1)} %shard_map.82.tiles_ref) | copy-start | bytes 3932164

commit v6 on v5

--- a/solution.py
+++ b/solution.py
@@ -627,11 +627,34 @@
     )(echoes, weights, replica, jnp.asarray(dft), jnp.asarray(twist), doppler, gate, owner)
 
 
-def rows_kernel(tiles_ref, out_ref, in_ref):
-    slots = out_ref.shape[0]
-    in_ref[...] = tiles_ref[...].reshape(8 * slots, 128).astype(F32)
-    for k in range(8):
-        out_ref[:, 128 * k : 128 * k + 128] = in_ref[pl.ds(k, slots, stride=8), :]
+PARTS = 4
+
+
+def rows_kernel(tiles_hbm, out_hbm, tiles_ref, wide_ref, out_ref, here, gone):
+    holders, slots = tiles_ref.shape[1], out_ref.shape[1]
+    loads = [
+        pltpu.make_async_copy(
+            tiles_hbm.at[pl.ds(part * holders, holders)], tiles_ref.at[part], here.at[part]
+        )
+        for part in range(PARTS)
+    ]
+    stores = [
+        pltpu.make_async_copy(
+            out_ref.at[part], out_hbm.at[pl.ds(part * slots, slots)], gone.at[part]
+        )
+        for part in range(PARTS)
+    ]
+    for load in loads:
+        load.start()
+    for part in range(PARTS):
+        loads[part].wait()
+        wide_ref[part] = tiles_ref[part].reshape(8 * slots, 128).astype(F32)
+        for k in range(8):
+            rows = wide_ref[part, pl.ds(k, slots, stride=8), :]
+            out_ref[part, :, 128 * k : 128 * k + 128] = rows
+        stores[part].start()
+    for store in stores:
+        store.wait()
 
 
 def params(mib, **more):
@@ -645,13 +668,21 @@
     capacity = 5
     rows = (x.reshape(1, tracks) for x in (track_doppler, track_gate, track_owner))
     received = tiles(echoes, beam_weights.reshape(32, 256), replica, *rows, owners)
+    hbm = pl.BlockSpec(memory_space=pltpu.HBM)
+    slots = owners * capacity // PARTS
     return pl.pallas_call(
         rows_kernel,
         out_shape=jax.ShapeDtypeStruct((owners * capacity, 1024), F32),
-        in_specs=[VMEM],
-        out_specs=VMEM,
-        scratch_shapes=[pltpu.VMEM((owners * capacity * 8, 128), F32)],
-        compiler_params=params(16),
+        in_specs=[hbm],
+        out_specs=hbm,
+        scratch_shapes=[
+            pltpu.VMEM((PARTS, owners // PARTS, capacity * 8, 128), BF16),
+            pltpu.VMEM((PARTS, slots * 8, 128), F32),
+            pltpu.VMEM((PARTS, slots, 1024), F32),
+            pltpu.SemaphoreType.DMA((PARTS,)),
+            pltpu.SemaphoreType.DMA((PARTS,)),
+        ],
+        compiler_params=params(60),
     )(received)
 
 

time: 82.8 us -> 81.9 us (0.989)
  local copies, waits for them, and re-layouts: 1.31 us -> 0 us
    unnamed x2 -> x0, local copies, waits for them, and re-layouts: 1.31 us -> none
where the time goes in v6:
time: 81.9 us; the launch traced here: 80.5 us
  Pallas kernels  80.5 us (98%)
    pallas_call x1, Pallas kernels, tiles(): pl.pallas_call(tiles_kernel, out_shape=jax.ShapeDtypeStruct((owners, ROWS...  77.8 us
    pallas_call x1, Pallas kernels, local(): pl.pallas_call(rows_kernel, out_shape=jax.ShapeDtypeStruct((owners * capa...  2.68 us

profile of v6, /device:TPU:1, one launch (start us, length us, event | category | flops | bytes accessed | tf_op | source)
XLA Modules:
  0.0 80.5 jit_solution(7413088428501175185)
XLA Ops:
  0.0 77.8 %shard_map.82.tiles_hbm = bf16[128,40,128]{2,1,0:T(8,128)(2,1)} custom-call(bf16[2,8,256,256]{3,2,1,0:T(8,128)(2,1)} %echo_hbm.1, f32[32,256]{1,0:T(8,128)} %bitcast.4, bf16[2,256]{1,0:T(2,128)(2,1)} %replica_hbm.1, bf16[512,512]{1,0:T(8,128)(2,1)} %constant.4.clone.dft_hbm, f32[2,8,256]{2,1,0:T(8,128)} %constant.5.clone.twist_hbm, s32[1,256]{1,0:T(1,128)} %bitcast.5, ...), custom_call_target="tpu_custom_call" | custom-call | flops 6000000000 | bytes 8388608 | tf_op jit(solution)/shard_map/pallas_call | solution.py:580
  77.8 2.7 %shard_map.83 = f32[640,1024]{1,0:T(8,128)} custom-call(bf16[128,40,128]{2,1,0:T(8,128)(2,1)} %shard_map.82.tiles_hbm), custom_call_target="tpu_custom_call" | custom-call | tf_op jit(solution)/shard_map/pallas_call | solution.py:673

commit v7 on v6

--- a/solution.py
+++ b/solution.py
@@ -523,8 +523,11 @@
             **at(owner // gates, lax.rem(owner, gates)),
         )
 
+    def turned(k):
+        return lax.rem(me + k // gates, 8) * gates + lax.rem(g + k, gates)
+
     def cut_and_send(step, carry):
-        near = [lax.rem(here + 1 + step * STEP + k, devices) for k in range(STEP)]
+        near = [turned(1 + step * STEP + k) for k in range(STEP)]
         for owner, part in zip(near, [cut_block(owner) for owner in near]):
             out_tile[owner] = part
         for owner in near:
@@ -534,7 +537,7 @@
     steps = (devices - 1) // STEP
     lax.fori_loop(0, steps, cut_and_send, 0)
     for k in range(1 + steps * STEP, devices):
-        owner = lax.rem(here + k, devices)
+        owner = turned(k)
         out_tile[owner] = cut_block(owner)
         tile(owner, here).start()
     tiles_ref[here] = cut_block(here)

time: 81.9 us -> 78.9 us (0.963); the launches traced: 80.5 us -> 78.7 us
  Pallas kernels: 80.5 us -> 78.7 us
    pallas_call x1, Pallas kernels: 77.8 us -> 76 us  [tiles(): pl.pallas_call(tiles_kernel, out_shape=jax.ShapeDtypeStruct((owners, ROWS...]
where the time goes in v7:
time: 78.9 us; the launch traced here: 78.7 us
  Pallas kernels  78.7 us (100%)
    pallas_call x1, Pallas kernels, tiles(): pl.pallas_call(tiles_kernel, out_shape=jax.ShapeDtypeStruct((owners, ROWS...  76 us
    pallas_call x1, Pallas kernels, local(): pl.pallas_call(rows_kernel, out_shape=jax.ShapeDtypeStruct((owners * capa...  2.68 us

profile of v7, /device:TPU:1, one launch (start us, length us, event | category | flops | bytes accessed | tf_op | source)
XLA Modules:
  0.0 78.7 jit_solution(10609463505886142869)
XLA Ops:
  0.0 76.0 %shard_map.82.tiles_hbm = bf16[128,40,128]{2,1,0:T(8,128)(2,1)} custom-call(bf16[2,8,256,256]{3,2,1,0:T(8,128)(2,1)} %echo_hbm.1, f32[32,256]{1,0:T(8,128)} %bitcast.4, bf16[2,256]{1,0:T(2,128)(2,1)} %replica_hbm.1, bf16[512,512]{1,0:T(8,128)(2,1)} %constant.4.clone.dft_hbm, f32[2,8,256]{2,1,0:T(8,128)} %constant.5.clone.twist_hbm, s32[1,256]{1,0:T(1,128)} %bitcast.5, ...), custom_call_target="tpu_custom_call" | custom-call | flops 6000000000 | bytes 8388608 | tf_op jit(solution)/shard_map/pallas_call | solution.py:583
  76.1 2.7 %shard_map.83 = f32[640,1024]{1,0:T(8,128)} custom-call(bf16[128,40,128]{2,1,0:T(8,128)(2,1)} %shard_map.82.tiles_hbm), custom_call_target="tpu_custom_call" | custom-call | tf_op jit(solution)/shard_map/pallas_call | solution.py:676

commit v8 on v7

--- a/solution.py
+++ b/solution.py
@@ -95,11 +95,7 @@
         ],
         axis=0,
     )
-    high = w.astype(BF16)
-    rest = w - high.astype(F32)
-    mid = rest.astype(BF16)
-    low = (rest - mid.astype(F32)).astype(BF16)
-    wide_ref[i] = sum(jnp.dot(part, spread, preferred_element_type=F32) for part in (low, mid, high))
+    wide_ref[i] = jnp.dot(w.astype(BF16), spread, preferred_element_type=F32)
 
 
 def pack_block(j, acc_ref, out_ref):
@@ -243,6 +239,7 @@
     out_strip,
     in_strip,
     all_weights,
+    float_weights,
     wide_ref,
     z_ref,
     acc_ref,
@@ -371,7 +368,7 @@
 
     loads[0].wait()
     for half in range(2):
-        weight_ref[half] = weights_ref[:, 128 * half : 128 * half + 128]
+        weight_ref[half] = weights_ref[:, 128 * half : 128 * half + 128].astype(BF16)
     turn(0)
     pl.semaphore_wait(barrier, 7 + gates - 1)
     for k in range(1, 8):
@@ -417,9 +414,10 @@
     make_taps(replica_ref, taps_ref)
     for k in range(1, 8):
         weight(me, peer(k)).wait_recv()
+    float_weights[...] = all_weights[...].astype(F32)
 
     def widen_step(i, carry):
-        widen(i, all_weights, wide_ref)
+        widen(i, float_weights, wide_ref)
         return carry
 
     lax.fori_loop(0, 32, widen_step, 0)
@@ -524,7 +522,7 @@
         )
 
     def turned(k):
-        return lax.rem(me + k // gates, 8) * gates + lax.rem(g + k, gates)
+        return lax.rem(me + k // gates, 8) * gates + lax.rem(g + 5 * k, gates)
 
     def cut_and_send(step, carry):
         near = [turned(1 + step * STEP + k) for k in range(STEP)]
@@ -594,11 +592,12 @@
             pltpu.VMEM((3, 1, 256), jnp.int32),
             pltpu.VMEM((1, owners * 5), jnp.int32),
             pltpu.SMEM((1, owners * 5), jnp.int32),
-            pltpu.VMEM((2, 32, 128), F32),
+            pltpu.VMEM((2, 32, 128), BF16),
             pltpu.VMEM((33 * UNITS, 8, 128), F32),
             pltpu.VMEM((owners, ROWS, 128), BF16),
             pltpu.VMEM((2, PAIRS, 8, 2, 2, 16, 256), BF16),
             pltpu.VMEM((2, PAIRS, 8, 2, 2, 16, 256), BF16),
+            pltpu.VMEM((8, 2, 32, 128), BF16),
             pltpu.VMEM((8, 2, 32, 128), F32),
             pltpu.VMEM((32, 256, 128), F32),
             pltpu.VMEM((256, 512), BF16),

time: 78.9 us -> 78 us (0.989)
  Pallas kernels: 78.7 us -> 77.6 us
    pallas_call x1, Pallas kernels: 76 us -> 75 us  [tiles(): pl.pallas_call(tiles_kernel, out_shape=jax.ShapeDtypeStruct((owners, ROWS...]
where the time goes in v8:
time: 78 us; the launch traced here: 77.6 us
  Pallas kernels  77.6 us (99%)
    pallas_call x1, Pallas kernels, tiles(): pl.pallas_call(tiles_kernel, out_shape=jax.ShapeDtypeStruct((owners, ROWS...  75 us
    pallas_call x1, Pallas kernels, local(): pl.pallas_call(rows_kernel, out_shape=jax.ShapeDtypeStruct((owners * capa...  2.68 us

profile of v8, /device:TPU:1, one launch (start us, length us, event | category | flops | bytes accessed | tf_op | source)
XLA Modules:
  0.0 77.6 jit_solution(17303365204307193918)
XLA Ops:
  0.0 75.0 %shard_map.82.tiles_hbm = bf16[128,40,128]{2,1,0:T(8,128)(2,1)} custom-call(bf16[2,8,256,256]{3,2,1,0:T(8,128)(2,1)} %echo_hbm.1, f32[32,256]{1,0:T(8,128)} %bitcast.4, bf16[2,256]{1,0:T(2,128)(2,1)} %replica_hbm.1, bf16[512,512]{1,0:T(8,128)(2,1)} %constant.4.clone.dft_hbm, f32[2,8,256]{2,1,0:T(8,128)} %constant.5.clone.twist_hbm, s32[1,256]{1,0:T(1,128)} %bitcast.5, ...), custom_call_target="tpu_custom_call" | custom-call | flops 6000000000 | bytes 8388608 | tf_op jit(solution)/shard_map/pallas_call | solution.py:581
  75.0 2.7 %shard_map.83 = f32[640,1024]{1,0:T(8,128)} custom-call(bf16[128,40,128]{2,1,0:T(8,128)(2,1)} %shard_map.82.tiles_hbm), custom_call_target="tpu_custom_call" | custom-call | tf_op jit(solution)/shard_map/pallas_call | solution.py:675
